TPU v7x, 128 devices: a whole 4x4x4 slice. The times are simulated.
128 devices in a mesh: dom: 32 (over y, x, core), rep: 4 (over z).
Axes of the slice: x: 4, y: 4, z: 4, core: 2. Of those that a mesh axis runs over, the one named last changes fastest.
Arguments:
- node_feat: bfloat16 [4, 8192, 512], P('rep', 'dom'), may hold values from -6 to 6
- edge_feat: bfloat16 [4, 65536, 512], P('rep', 'dom'), may hold values from -6 to 6
- node_cot: bfloat16 [4, 8192, 512], P('rep', 'dom'), may hold values from -6 to 6
- edge_cot: bfloat16 [4, 65536, 512], P('rep', 'dom'), may hold values from -6 to 6
- edge_in_w: bfloat16 [1536, 512], replicated, may hold values from -0.15625 to 0.15625
- edge_bias: float32 [512], replicated, may hold values from -3 to 3
- edge_out_w: bfloat16 [512, 512], replicated, may hold values from -0.25 to 0.25
- edge_gain: float32 [512], replicated, may hold values from 0.25 to 1.75
- node_in_w: bfloat16 [1024, 512], replicated, may hold values from -0.1875 to 0.1875
- node_bias: float32 [512], replicated, may hold values from -3 to 3
- node_out_w: bfloat16 [512, 512], replicated, may hold values from -0.25 to 0.25
- node_gain: float32 [512], replicated, may hold values from 0.25 to 1.75
- senders: int32 [65536], P('dom'), may hold values from 0 to 1279, as said below
- receivers: int32 [65536], P('dom'), may hold values from 0 to 255
- send_rows: int32 [1024, 32], P('dom'), may hold values from 0 to 255
- live_edges: int32 [32], P('dom'), may hold values from 1 to 2048, 40960 in all
Outputs:
- grad_nodes: bfloat16 [4, 8192, 512], P('rep', 'dom')
- grad_edges: bfloat16 [4, 65536, 512], P('rep', 'dom')
- grad_matrices: float32 [3584, 512], P('dom')
- grad_vectors: float32 [4, 512], replicated
Inputs may be any that keep to these rules, and one draw needn't show every extreme that they name: `senders`: rows below 256 are local nodes; row 256 + q * 32 + j is slot j of the list that region q sends to this region. `receivers`: A local node of the edge's own region. `send_rows`: row q * 32 + p lists local nodes of region q that region p receives; nodes may repeat. `live_edges`: some region uses all its slots; the used slots come first.
All inputs are finite; a program needn't handle non-finite values. No bound on the sum of `live_edges` on one device may be relied on, other than what follows from the above.
Results may differ from a plain program's by a relative error of at most 0.014.
Values may be sent and summed in bfloat16 or wider, within the bound.
No kernel may reach another device: no remote copies, remote signals or barrier semaphores. Data moves between devices by JAX's collectives and lax.ppermute only.
A program may use at most 192 MiB of HBM per device.

v0:
```python
import jax
import jax.numpy as jnp
from jax import lax
from jax.experimental import pallas as pl
from jax.experimental.pallas import tpu as pltpu
from jax.sharding import PartitionSpec as P

epsilon = 1e-05
f32 = jnp.float32
bf16 = jnp.bfloat16
NT = (((1,), (1,)), ((), ()))
TN = (((0,), (0,)), ((), ()))
VMEM_LIMIT = 58 * 1024 * 1024
CHUNK = 1024
DEAD = 0x10000


def mm(a, b):
    return jnp.dot(a, b, preferred_element_type=f32)


def mm_nt(a, b):
    return lax.dot_general(a, b, NT, preferred_element_type=f32)


def mm_tn(a, b):
    return lax.dot_general(a, b, TN, preferred_element_type=f32)


def params():
    return pltpu.CompilerParams(vmem_limit_bytes=VMEM_LIMIT)


def cost(flops, moved):
    return pl.CostEstimate(flops=flops, bytes_accessed=moved, transcendentals=0)


def one_hot_t(row, first, count):
    ids = lax.broadcasted_iota(jnp.int32, (count, row.shape[1]), 0) + first
    return jnp.where(ids == row, 1.0, 0.0).astype(bf16)


def columns(row):
    k = row.shape[1]
    parts = [
        jnp.transpose(jnp.broadcast_to(row[:, i : i + 128], (128, 128))) for i in range(0, k, 128)
    ]
    return jnp.concatenate(parts, axis=0)


def one_hot(column, first, count):
    lane = lax.broadcasted_iota(jnp.int32, column.shape, 1)
    parts = [
        jnp.where(column == lane + (first + i), 1.0, 0.0).astype(bf16)
        for i in range(0, count, 128)
    ]
    return jnp.concatenate(parts, axis=1)


def sigmoid(value):
    return 0.5 * jnp.tanh(0.5 * value) + 0.5


def normalise(value):
    center = value - jnp.mean(value, axis=-1, keepdims=True)
    recip = lax.rsqrt(jnp.mean(center * center, axis=-1, keepdims=True) + epsilon)
    return center * recip, recip


def norm_backward(upper, normed, recip):
    return recip * (
        upper
        - jnp.mean(upper, axis=-1, keepdims=True)
        - normed * jnp.mean(upper * normed, axis=-1, keepdims=True)
    )


def send_kernel(rows_ref, nodes_ref, out_ref):
    n = nodes_ref.shape[0]
    regions, cap = rows_ref.shape
    listed = jnp.transpose(rows_ref[...])
    lane = lax.broadcasted_iota(jnp.int32, (cap, n), 1)
    picks = jnp.concatenate(
        [jnp.where(listed[:, q : q + 1] == lane, 1.0, 0.0).astype(bf16) for q in range(regions)],
        axis=0,
    )
    out_ref[...] = mm(picks, nodes_ref[...]).astype(bf16)


def before_kernel(
    snd_ref,
    rcv_ref,
    edges_ref,
    nodes_ref,
    ein_ref,
    ebias_ref,
    part_ref,
    local_ref,
    far_ref,
    rcv_t_ref,
    rcv_n_ref,
    table_scr,
):
    n, width = nodes_ref.shape
    remote = far_ref.shape[1]
    c = pl.program_id(0)

    @pl.when(c == 0)
    def _():
        table_scr[...] = mm(nodes_ref[...], ein_ref[2 * width :, :]).astype(bf16)

    snd = columns(snd_ref[pl.ds(c, 1), :])
    row = rcv_ref[pl.ds(c, 1), :]
    rcv = columns(row)
    near = one_hot(jnp.bitwise_and(rcv, DEAD - 1), 0, n)
    local_ref[...] = mm(one_hot(snd, 0, n), nodes_ref[...]).astype(bf16)
    far_ref[...] = one_hot(snd, n, remote)
    rcv_t_ref[...] = one_hot_t(row, 0, n)
    rcv_n_ref[...] = one_hot(rcv, 0, n)
    part_ref[...] = (
        mm(edges_ref[...], ein_ref[:width, :]) + mm(near, table_scr[...]) + ebias_ref[...]
    )


def deal(core, mats_ref, vecs, mine_ref, send_ref):
    blocks = mine_ref.shape[0]
    regions = 2 * blocks
    share, width = mats_ref.shape[0] // regions, mats_ref.shape[1]
    tail = jnp.concatenate(
        [vec[:, j : j + 128] for vec in vecs for j in range(0, width, 128)], axis=0
    ).astype(bf16)
    for out_ref, parity in ((mine_ref, core), (send_ref, 1 - core)):
        for i in range(blocks):
            at = pl.multiple_of((2 * i + parity) * share, 16)
            rows = mats_ref[pl.ds(at, share), :]
            for j in range(width // 128):
                out_ref[i, j * share : (j + 1) * share] = rows[:, j * 128 : (j + 1) * 128]
            out_ref[i, width // 128 * share :] = tail


def main_kernel(
    place_ref,
    egain_ref,
    nbias_ref,
    ngain_ref,
    part_hbm,
    local_hbm,
    far_hbm,
    rcv_t_hbm,
    rcv_n_hbm,
    cot_hbm,
    edges_hbm,
    nodes_hbm,
    ncot_hbm,
    arrived_hbm,
    ein_hbm,
    eout_hbm,
    nin_hbm,
    nout_hbm,
    hg_hbm,
    base_hbm,
    mine_hbm,
    send_hbm,
    part_ref,
    local_ref,
    far_ref,
    rcv_t_ref,
    rcv_n_ref,
    cot_ref,
    edges_ref,
    nodes_ref,
    ncot_ref,
    arrived_ref,
    ws_ref,
    wr_ref,
    eout_ref,
    nin_ref,
    nout_ref,
    hg_ref,
    base_ref,
    mine_ref,
    send_ref,
    act_ref,
    slope_ref,
    normed_ref,
    recip_ref,
    mats_ref,
    chunk_sems,
    sems,
    out_sems,
):
    count, width = part_ref.shape
    n = nodes_ref.shape[0]
    chunk = min(CHUNK, count)
    n_chunks = count // chunk
    streams = [
        (far_hbm, far_ref),
        (local_hbm, local_ref),
        (part_hbm, part_ref),
        (rcv_n_hbm, rcv_n_ref),
        (cot_hbm, cot_ref),
        (edges_hbm, edges_ref),
    ]

    def stream(k, c):
        src, dst = streams[k]
        at = pl.ds(c * chunk, chunk)
        return pltpu.make_async_copy(src.at[at], dst.at[at], chunk_sems.at[k, c])

    singles = [
        (arrived_hbm, arrived_ref),
        (ein_hbm.at[pl.ds(width, width)], ws_ref),
        (eout_hbm, eout_ref),
        (rcv_t_hbm, rcv_t_ref),
        (nodes_hbm, nodes_ref),
        (nin_hbm, nin_ref),
        (nout_hbm, nout_ref),
        (ncot_hbm, ncot_ref),
        (ein_hbm.at[pl.ds(2 * width, width)], wr_ref),
    ]
    single = [pltpu.make_async_copy(src, dst, sems.at[k]) for k, (src, dst) in enumerate(singles)]
    stream(0, 0).start()
    single[0].start()
    stream(1, 0).start()
    single[1].start()
    stream(2, 0).start()
    single[2].start()
    single[3].start()
    for c in range(1, n_chunks):
        for k in range(3):
            stream(k, c).start()
    for k in range(4, 8):
        single[k].start()
    for c in range(n_chunks):
        for k in range(3, 6):
            stream(k, c).start()
    single[8].start()

    egain = egain_ref[...]
    for c in range(n_chunks):
        here = pl.ds(c * chunk, chunk)
        stream(0, c).wait()
        stream(1, c).wait()
        if c == 0:
            single[0].wait()
        picked = local_ref[here, :] + mm(far_ref[here, :], arrived_ref[...]).astype(bf16)
        local_ref[here, :] = picked
        stream(2, c).wait()
        if c == 0:
            single[1].wait()
        hidden = part_ref[here, :] + mm(picked, ws_ref[...])
        s = sigmoid(hidden)
        act = (hidden * s).astype(bf16)
        act_ref[here, :] = act
        slope_ref[here, :] = s * (1.0 + hidden * (1.0 - s))
        if c == 0:
            single[2].wait()
        normed, recip = normalise(mm(act, eout_ref[...]))
        normed_ref[here, :] = normed
        recip_ref[here, :] = recip
        message = (normed * egain).astype(bf16)
        if c == 0:
            single[3].wait()
        term = mm(rcv_t_ref[:, c * chunk : (c + 1) * chunk], message)
        agg = term if c == 0 else agg + term

    for k in range(4, 8):
        single[k].wait()
    nodes = nodes_ref[...]
    agg = agg.astype(bf16)
    hidden = mm(nodes, nin_ref[:width, :]) + mm(agg, nin_ref[width:, :]) + nbias_ref[...]
    s = sigmoid(hidden)
    act = (hidden * s).astype(bf16)
    normed, recip = normalise(mm(act, nout_ref[...]))
    upstream = ncot_ref[...].astype(f32)
    pre_grad = norm_backward(upstream * ngain_ref[...], normed, recip).astype(bf16)
    hidden_grad = (mm_nt(pre_grad, nout_ref[...]) * (s * (1.0 + hidden * (1.0 - s)))).astype(bf16)
    agg_grad = mm_nt(hidden_grad, nin_ref[width:, :]).astype(bf16)
    vecs = [
        None,
        None,
        jnp.sum(hidden_grad.astype(f32), axis=0, keepdims=True),
        jnp.sum(upstream * normed, axis=0, keepdims=True),
    ]

    for c in range(n_chunks):
        here = pl.ds(c * chunk, chunk)
        stream(3, c).wait()
        picks = rcv_n_ref[here, :]
        live = jnp.max(picks.astype(f32), axis=1, keepdims=True) > 0.5
        gathered = mm(picks, agg_grad)
        stream(4, c).wait()
        message_grad = jnp.where(live, cot_ref[here, :].astype(f32) + gathered, 0.0)
        edge_normed = normed_ref[here, :]
        term = jnp.sum(message_grad * edge_normed, axis=0, keepdims=True)
        vecs[1] = term if c == 0 else vecs[1] + term
        edge_pre_grad = norm_backward(
            message_grad * egain, edge_normed, recip_ref[here, :]
        ).astype(bf16)
        edge_grad = (mm_nt(edge_pre_grad, eout_ref[...]) * slope_ref[here, :]).astype(bf16)
        hg_ref[here, :] = edge_grad
        pltpu.make_async_copy(hg_ref.at[here], hg_hbm.at[here], out_sems.at[c]).start()
        term = jnp.sum(edge_grad.astype(f32), axis=0, keepdims=True)
        vecs[0] = term if c == 0 else vecs[0] + term
        stream(5, c).wait()
        terms = [
            mm_tn(edges_ref[here, :], edge_grad),
            mm_tn(local_ref[here, :], edge_grad),
            mm_tn(act_ref[here, :], edge_pre_grad),
            mm(rcv_t_ref[:, c * chunk : (c + 1) * chunk], edge_grad),
        ]
        sums = terms if c == 0 else [a + b for a, b in zip(sums, terms)]

    single[8].wait()
    received = sums[3].astype(bf16)
    base_ref[...] = (
        upstream + mm_nt(hidden_grad, nin_ref[:width, :]) + mm_nt(received, wr_ref[...])
    )
    base_copy = pltpu.make_async_copy(base_ref, base_hbm, out_sems.at[n_chunks])
    base_copy.start()
    mats_ref[:width, :] = sums[0].astype(bf16)
    mats_ref[width : 2 * width, :] = sums[1].astype(bf16)
    mats_ref[2 * width : 3 * width, :] = mm_tn(nodes, received).astype(bf16)
    mats_ref[3 * width : 4 * width, :] = sums[2].astype(bf16)
    mats_ref[4 * width : 5 * width, :] = mm_tn(nodes, hidden_grad).astype(bf16)
    mats_ref[5 * width : 6 * width, :] = mm_tn(agg, hidden_grad).astype(bf16)
    mats_ref[6 * width :, :] = mm_tn(act, pre_grad).astype(bf16)
    deal(place_ref[0], mats_ref, vecs, mine_ref, send_ref)
    last = [
        pltpu.make_async_copy(send_ref, send_hbm, out_sems.at[n_chunks + 1]),
        pltpu.make_async_copy(mine_ref, mine_hbm, out_sems.at[n_chunks + 2]),
    ]
    for copy in last:
        copy.start()
    for c in range(n_chunks):
        here = pl.ds(c * chunk, chunk)
        pltpu.make_async_copy(hg_ref.at[here], hg_hbm.at[here], out_sems.at[c]).wait()
    base_copy.wait()
    for copy in last:
        copy.wait()


def senders_kernel(snd_ref, hg_ref, ws_ref, base_ref, sent_ref, out_ref):
    n, width = base_ref.shape
    remote = sent_ref.shape[0]
    snd = snd_ref[...]
    local = mm(one_hot_t(snd, 0, n), hg_ref[...]).astype(bf16)
    out_ref[...] = base_ref[...] + mm_nt(local, ws_ref[...])
    tile = 256 if remote % 256 == 0 else remote

    @pl.loop(0, remote // tile)
    def _(i):
        at = pl.multiple_of(i * tile, tile)
        part = mm(one_hot_t(snd, n + at, tile), hg_ref[...]).astype(bf16)
        sent_ref[pl.ds(at, tile), :] = part


def edges_kernel(hg_ref, cot_ref, w_ref, out_ref):
    out_ref[...] = (cot_ref[...].astype(f32) + mm_nt(hg_ref[...], w_ref[...])).astype(bf16)


def finish_kernel(rows_ref, returned_ref, ws_ref, base_ref, out_ref):
    n, width = base_ref.shape
    own = mm(one_hot_t(rows_ref[...], 0, n), returned_ref[...]).astype(bf16)
    out_ref[...] = (base_ref[...] + mm_nt(own, ws_ref[...])).astype(bf16)


def over_chips_kernel(parts_ref, own_ref, sent_ref):
    total = jnp.sum(parts_ref[...].astype(f32), axis=0)
    own_ref[...] = total
    sent_ref[...] = total.astype(bf16)


def join_kernel(*refs):
    mats_ref, vecs_ref = refs[-2:]
    share, width = mats_ref.shape
    total = refs[0][...]
    for ref in refs[1:-2]:
        total = total + ref[...].astype(f32)
    slabs = width // 128
    for j in range(slabs):
        mats_ref[:, j * 128 : (j + 1) * 128] = total[j * share : (j + 1) * share]
        for k in range(4):
            at = slabs * share + k * slabs + j
            vecs_ref[k : k + 1, j * 128 : (j + 1) * 128] = total[at : at + 1]


def shards(
    node_feat,
    edge_feat,
    node_cot,
    edge_cot,
    edge_in_w,
    edge_bias,
    edge_out_w,
    edge_gain,
    node_in_w,
    node_bias,
    node_out_w,
    node_gain,
    senders,
    receivers,
    send_rows,
    live_edges,
):
    nodes = node_feat[0]
    edges = edge_feat[0]
    cots = edge_cot[0]
    n, width = nodes.shape
    count = edges.shape[0]
    regions, cap = send_rows.shape
    remote = regions * cap
    chunk = min(CHUNK, count)
    n_chunks = count // chunk
    rows = edge_in_w.shape[0] + edge_out_w.shape[0] + node_in_w.shape[0] + node_out_w.shape[0]
    share = rows // regions
    chips = regions // 2
    reps = lax.axis_size("rep")
    core = lax.rem(lax.axis_index("dom"), 2).reshape(1)
    smem = pl.BlockSpec(memory_space=pltpu.SMEM)
    vmem = pl.BlockSpec(memory_space=pltpu.VMEM)
    shape = jax.ShapeDtypeStruct

    def whole(shape):
        return pl.BlockSpec(shape, lambda i: (0,) * len(shape))

    def rows_of(width):
        return pl.BlockSpec((chunk, width), lambda i: (i, 0))

    outgoing = pl.pallas_call(
        send_kernel,
        out_shape=shape((remote, width), bf16),
        compiler_params=params(),
        cost_estimate=cost(2 * remote * n * width, 4 * remote * width),
    )(send_rows, nodes)
    arrived = lax.all_to_all(
        outgoing.reshape(regions, cap, width), "dom", split_axis=0, concat_axis=0, tiled=True
    ).reshape(remote, width)

    live = jnp.arange(count, dtype=jnp.int32) < live_edges[0]
    rcv = jnp.where(live, receivers, receivers + DEAD).reshape(n_chunks, chunk)
    hidden_part, local, far, rcv_t, rcv_n = pl.pallas_call(
        before_kernel,
        grid=(n_chunks,),
        in_specs=[
            whole((n_chunks, chunk)),
            whole((n_chunks, chunk)),
            rows_of(width),
            whole((n, width)),
            whole(edge_in_w.shape),
            whole((1, width)),
        ],
        out_specs=[
            rows_of(width),
            rows_of(width),
            rows_of(remote),
            pl.BlockSpec((n, chunk), lambda i: (0, i)),
            rows_of(n),
        ],
        out_shape=[
            shape((count, width), f32),
            shape((count, width), bf16),
            shape((count, remote), bf16),
            shape((n, count), bf16),
            shape((count, n), bf16),
        ],
        scratch_shapes=[pltpu.VMEM((n, width), bf16)],
        compiler_params=params(),
        cost_estimate=cost(6_000_000_000, 16_000_000),
    )(
        senders.reshape(n_chunks, chunk),
        rcv,
        edges,
        nodes,
        edge_in_w,
        edge_bias.reshape(1, width),
    )

    hbm = pl.BlockSpec(memory_space=pl.ANY)
    slab = (share * width + 4 * width) // 128
    dealt = (chips, slab, 128)
    hidden_grad, base, mine, to_other = pl.pallas_call(
        main_kernel,
        in_specs=[smem, vmem, vmem, vmem] + [hbm] * 14,
        out_specs=[hbm] * 4,
        out_shape=[
            shape((count, width), bf16),
            shape((n, width), f32),
            shape(dealt, bf16),
            shape(dealt, bf16),
        ],
        scratch_shapes=[
            pltpu.VMEM((count, width), f32),
            pltpu.VMEM((count, width), bf16),
            pltpu.VMEM((count, remote), bf16),
            pltpu.VMEM((n, count), bf16),
            pltpu.VMEM((count, n), bf16),
            pltpu.VMEM((count, width), bf16),
            pltpu.VMEM((count, width), bf16),
            pltpu.VMEM((n, width), bf16),
            pltpu.VMEM((n, width), bf16),
            pltpu.VMEM((remote, width), bf16),
            pltpu.VMEM((width, width), bf16),
            pltpu.VMEM((width, width), bf16),
            pltpu.VMEM(edge_out_w.shape, bf16),
            pltpu.VMEM(node_in_w.shape, bf16),
            pltpu.VMEM(node_out_w.shape, bf16),
            pltpu.VMEM((count, width), bf16),
            pltpu.VMEM((n, width), f32),
            pltpu.VMEM(dealt, bf16),
            pltpu.VMEM(dealt, bf16),
            pltpu.VMEM((count, width), bf16),
            pltpu.VMEM((count, width), f32),
            pltpu.VMEM((count, width), f32),
            pltpu.VMEM((count, 1), f32),
            pltpu.VMEM((rows, width), bf16),
            pltpu.SemaphoreType.DMA((6, n_chunks)),
            pltpu.SemaphoreType.DMA((9,)),
            pltpu.SemaphoreType.DMA((n_chunks + 3,)),
        ],
        compiler_params=params(),
        cost_estimate=cost(16_000_000_000, 30_000_000),
    )(
        core,
        edge_gain.reshape(1, width),
        node_bias.reshape(1, width),
        node_gain.reshape(1, width),
        hidden_part,
        local,
        far,
        rcv_t,
        rcv_n,
        cots,
        edges,
        nodes,
        node_cot[0],
        arrived,
        edge_in_w,
        edge_out_w,
        node_in_w,
        node_out_w,
    )

    one_block = pl.BlockSpec((width, width), lambda i: (1, 0))
    from_other = lax.ppermute(to_other, "dom", [(i, i ^ 1) for i in range(regions)])
    chip_sum = (mine.astype(f32) + from_other.astype(f32)).astype(bf16)
    chip_sum, hidden_grad = lax.optimization_barrier((chip_sum, hidden_grad))
    by_chip = lax.all_to_all(
        chip_sum,
        "dom",
        split_axis=0,
        concat_axis=0,
        axis_index_groups=[list(range(c, regions, 2)) for c in range(2)],
        tiled=True,
    )
    sent, base = pl.pallas_call(
        senders_kernel,
        grid=(1,),
        in_specs=[vmem, vmem, one_block, vmem],
        out_shape=(shape((remote, width), bf16), shape((n, width), f32)),
        compiler_params=params(),
        cost_estimate=cost(1000, 1000),
    )(senders.reshape(1, count), hidden_grad, edge_in_w, base)
    grad_edges = pl.pallas_call(
        edges_kernel,
        grid=(n_chunks,),
        in_specs=[
            rows_of(width),
            rows_of(width),
            pl.BlockSpec((width, width), lambda i: (0, 0)),
        ],
        out_specs=rows_of(width),
        out_shape=shape((count, width), bf16),
        compiler_params=params(),
        cost_estimate=cost(1000, 1000),
    )(hidden_grad, cots, edge_in_w)

    by_chip, sent, grad_edges = lax.optimization_barrier((by_chip, sent, grad_edges))
    returned = lax.all_to_all(
        sent.reshape(regions, cap, width), "dom", split_axis=0, concat_axis=0, tiled=True
    ).reshape(remote, width)
    total, total_bf16 = pl.pallas_call(
        over_chips_kernel,
        out_shape=(shape((slab, 128), f32), shape((slab, 128), bf16)),
        compiler_params=params(),
        cost_estimate=cost(1_000_000, 2_000_000),
    )(by_chip)
    totals = [total] + [
        lax.ppermute(total_bf16, "rep", [(i, (i + k) % reps) for i in range(reps)])
        for k in range(1, reps)
    ]
    grad_nodes = pl.pallas_call(
        finish_kernel,
        grid=(1,),
        in_specs=[vmem, vmem, one_block, vmem],
        out_shape=shape((n, width), bf16),
        compiler_params=params(),
        cost_estimate=cost(1000, 1000),
    )(send_rows.reshape(1, remote), returned, edge_in_w, base)
    own_rows, vector_total = pl.pallas_call(
        join_kernel,
        out_shape=(shape((share, width), f32), shape((4, width), f32)),
        compiler_params=params(),
    )(*totals)
    return (grad_nodes[None], grad_edges[None], own_rows, vector_total)


def solution(mesh):
    in_specs = (
        P("rep", "dom", None),
        P("rep", "dom", None),
        P("rep", "dom", None),
        P("rep", "dom", None),
        P(),
        P(),
        P(),
        P(),
        P(),
        P(),
        P(),
        P(),
        P("dom"),
        P("dom"),
        P("dom", None),
        P("dom"),
    )
    out_specs = (P("rep", "dom", None), P("rep", "dom", None), P("dom", None), P())
    return jax.shard_map(shards, mesh=mesh, in_specs=in_specs, out_specs=out_specs, check_vma=False)
```

profile of v0, /device:TPU:1, one launch (start us, length us, event | category | flops | bytes accessed | tf_op | source)
XLA Modules:
  0.0 121.6 jit_solution(5435136500532349759)
XLA Ops:
  0.7 2.6 %shard_map.184 = bf16[1024,512]{1,0:T(8,128)(2,1)} custom-call(s32[32,32]{1,0:T(8,128)} %rows_ref.1, bf16[256,512]{1,0:T(8,128)(2,1)} %bitcast.25), custom_call_target="tpu_custom_call" | custom-call | flops 268435456 | bytes 2097152 | tf_op jit(solution)/shard_map/pallas_call | solution.py:430
  3.2 8.6 %all-to-all-start = ((bf16[32,32,512]{2,1,0:T(8,128)(2,1)}), bf16[32,32,512]{2,1,0:T(8,128)(2,1)S(1)}, u32[]{:S(2)}, u32[]{:S(2)}) async-start(bf16[32,32,512]{2,1,0:T(8,128)(2,1)} %bitcast.18), calls=%async_computation | async-start | bytes 2097152 | tf_op jit(solution)/shard_map/all_to_all | solution.py:436
  13.7 8.1 %shard_map.183 = (f32[2048,512]{1,0:T(8,128)}, bf16[2048,512]{1,0:T(8,128)(2,1)}, bf16[2048,1024]{1,0:T(8,128)(2,1)}, bf16[256,2048]{1,0:T(8,128)(2,1)}, bf16[2048,256]{1,0:T(8,128)(2,1)}) custom-call(s32[2,1024]{1,0:T(2,128)} %reshape.52.snd_ref, s32[2,1024]{1,0:T(2,128)} %reshape.53.rcv_ref, bf16[2048,512]{1,0:T(8,128)(2,1)} %bitcast.30, ...), custom_call_target="tpu_custom_call" | custom-call | flops 6000000000 | bytes 16000000 | tf_op jit(solution)/shard_map/pallas_call | solution.py:442
  21.9 7.1 %all-to-all-done = bf16[32,32,512]{2,1,0:T(8,128)(2,1)S(1)} async-done(((bf16[32,32,512]{2,1,0:T(8,128)(2,1)}), bf16[32,32,512]{2,1,0:T(8,128)(2,1)S(1)}, u32[]{:S(2)}, u32[]{:S(2)}) %all-to-all-start) | async-done | bytes 1048608 | tf_op jit(solution)/shard_map/all_to_all | solution.py:436
  29.0 1.0 copy-done.2
  30.0 24.0 %shard_map.185 = (bf16[2048,512]{1,0:T(8,128)(2,1)}, f32[256,512]{1,0:T(8,128)}, bf16[16,464,128]{2,1,0:T(8,128)(2,1)}, bf16[16,464,128]{2,1,0:T(8,128)(2,1)}) custom-call(s32[1]{0:T(128)} %bitcast.place_ref, f32[1,512]{1,0:T(1,128)} %bitcast.34, f32[1,512]{1,0:T(1,128)} %bitcast.35, f32[1,512]{1,0:T(1,128)} %bitcast.36, ...), custom_call_target="tpu_custom_call" | custom-call | flops 16000000000 | bytes 30000000 | tf_op jit(solution)/shard_map/pallas_call | solution.py:482
  54.5 3.7 %collective-permute-done = bf16[16,464,128]{2,1,0:T(8,128)(2,1)S(1)} collective-permute-done((bf16[16,464,128]{2,1,0:T(8,128)(2,1)}, bf16[16,464,128]{2,1,0:T(8,128)(2,1)S(1)}, u32[]{:S(2)}, u32[]{:S(2)}) %collective-permute-start) | collective-permute-done | bytes 1900576 | tf_op jit(solution)/shard_map/ppermute | solution.py:545
  58.2 3.4 %add_convert_fusion = bf16[16,464,128]{2,1,0:T(8,128)(2,1)} fusion(bf16[16,464,128]{2,1,0:T(8,128)(2,1)S(1)} %collective-permute-done, bf16[16,464,128]{2,1,0:T(8,128)(2,1)} %get-tuple-element.29), kind=kLoop, calls=%fused_computation | loop fusion | flops 3801088 | bytes 5701632 | tf_op jit(solution)/shard_map/convert_element_type | solution.py:546
  61.6 3.7 %all-to-all-start.1 = ((bf16[16,464,128]{2,1,0:T(8,128)(2,1)}), bf16[16,464,128]{2,1,0:T(8,128)(2,1)S(1)}, u32[]{:S(2)}, u32[]{:S(2)}) async-start(bf16[16,464,128]{2,1,0:T(8,128)(2,1)} %add_convert_fusion), calls=%async_computation.1 | async-start | bytes 3801088 | tf_op jit(solution)/shard_map/all_to_all | solution.py:548
  65.4 4.2 %shard_map.187 = bf16[2048,512]{1,0:T(8,128)(2,1)} custom-call(bf16[2048,512]{1,0:T(8,128)(2,1)} %get-tuple-element.33.hg_ref, bf16[2048,512]{1,0:T(8,128)(2,1)} %bitcast.21, bf16[1536,512]{1,0:T(8,128)(2,1)} %ws_ref.3), custom_call_target="tpu_custom_call" | custom-call | flops 1000 | bytes 1000 | tf_op jit(solution)/shard_map/pallas_call | solution.py:564
  69.5 6.6 %shard_map.186 = (bf16[1024,512]{1,0:T(8,128)(2,1)}, f32[256,512]{1,0:T(8,128)}) custom-call(s32[1,2048]{1,0:T(1,128)} %bitcast.29, bf16[2048,512]{1,0:T(8,128)(2,1)} %get-tuple-element.33.hg_ref, bf16[1536,512]{1,0:T(8,128)(2,1)} %ws_ref.3, f32[256,512]{1,0:T(8,128)} %get-tuple-element.34.base_ref), custom_call_target="tpu_custom_call" | custom-call | flops 1000 | bytes 1000 | tf_op jit(solution)/shard_map/pallas_call | solution.py:556
  76.1 19.5 %all-to-all-done.1.parts_ref = bf16[16,464,128]{2,1,0:T(8,128)(2,1)S(1)} async-done(((bf16[16,464,128]{2,1,0:T(8,128)(2,1)}), bf16[16,464,128]{2,1,0:T(8,128)(2,1)S(1)}, u32[]{:S(2)}, u32[]{:S(2)}) %all-to-all-start.1) | async-done | bytes 1900576 | tf_op jit(solution)/shard_map/all_to_all | solution.py:548
  95.7 4.8 %all-to-all-start.2 = ((bf16[32,32,512]{2,1,0:T(8,128)(2,1)}), bf16[32,32,512]{2,1,0:T(8,128)(2,1)S(1)}, u32[]{:S(2)}, u32[]{:S(2)}) async-start(bf16[32,32,512]{2,1,0:T(8,128)(2,1)} %bitcast.24), calls=%async_computation.2 | async-start | bytes 2097152 | tf_op jit(solution)/shard_map/all_to_all | solution.py:579
  100.5 2.5 %shard_map.189 = (f32[464,128]{1,0:T(8,128)}, bf16[464,128]{1,0:T(8,128)(2,1)}) custom-call(bf16[16,464,128]{2,1,0:T(8,128)(2,1)} %copy-done), custom_call_target="tpu_custom_call" | custom-call | flops 1000000 | bytes 2000000 | tf_op jit(solution)/shard_map/pallas_call | solution.py:582
  102.9 1.6 %collective-permute-start.1 = (bf16[464,128]{1,0:T(8,128)(2,1)}, bf16[464,128]{1,0:T(8,128)(2,1)S(1)}, u32[]{:S(2)}, u32[]{:S(2)}) collective-permute-start(bf16[464,128]{1,0:T(8,128)(2,1)} %get-tuple-element.41), channel_id=1, source_target_pairs={{0,1},{1,2},{2,3},{3,0},{4,5},{5,6},{6,7},{7,4},{8,9},{9,10},{10,1... | collective-permute-start | bytes 356360 | tf_op jit(solution)/shard_map/ppermute | solution.py:589
  104.6 3.3 %collective-permute-start.2 = (bf16[464,128]{1,0:T(8,128)(2,1)}, bf16[464,128]{1,0:T(8,128)(2,1)S(1)}, u32[]{:S(2)}, u32[]{:S(2)}) collective-permute-start(bf16[464,128]{1,0:T(8,128)(2,1)} %get-tuple-element.41), channel_id=1, source_target_pairs={{0,2},{1,3},{2,0},{3,1},{4,6},{5,7},{6,4},{7,5},{8,10},{9,11},{10,... | collective-permute-start | bytes 356360 | tf_op jit(solution)/shard_map/ppermute | solution.py:589
  107.9 0.7 collective-permute-start.3
  108.6 0.7 reshape.47.rows_ref
  109.3 1.0 collective-permute-done.1.refs_1_
  110.3 3.4 %collective-permute-done.2.refs_2_ = bf16[464,128]{1,0:T(8,128)(2,1)S(1)} collective-permute-done((bf16[464,128]{1,0:T(8,128)(2,1)}, bf16[464,128]{1,0:T(8,128)(2,1)S(1)}, u32[]{:S(2)}, u32[]{:S(2)}) %collective-permute-start.2) | collective-permute-done | bytes 118816 | tf_op jit(solution)/shard_map/ppermute | solution.py:589
  114.4 1.9 %shard_map.190 = (f32[112,512]{1,0:T(8,128)}, f32[4,512]{1,0:T(4,128)}) custom-call(f32[464,128]{1,0:T(8,128)} %get-tuple-element.40.refs_0_, bf16[464,128]{1,0:T(8,128)(2,1)} %copy-done.3, bf16[464,128]{1,0:T(8,128)(2,1)} %copy-done.4, bf16[464,128]{1,0:T(8,128)(2,1)} %copy-done.5), custom_call_target="tpu_custom_call" | custom-call | tf_op jit(solution)/shard_map/pallas_call | solution.py:600
  116.2 1.5 %all-to-all-done.2 = bf16[32,32,512]{2,1,0:T(8,128)(2,1)S(1)} async-done(((bf16[32,32,512]{2,1,0:T(8,128)(2,1)}), bf16[32,32,512]{2,1,0:T(8,128)(2,1)S(1)}, u32[]{:S(2)}, u32[]{:S(2)}) %all-to-all-start.2) | async-done | bytes 1048608 | tf_op jit(solution)/shard_map/all_to_all | solution.py:579
  117.7 1.0 copy-done.1
  118.7 2.9 %shard_map.188 = bf16[256,512]{1,0:T(8,128)(2,1)} custom-call(s32[1,1024]{1,0:T(1,128)} %reshape.47.rows_ref, bf16[1024,512]{1,0:T(8,128)(2,1)} %bitcast.19, bf16[1536,512]{1,0:T(8,128)(2,1)} %ws_ref.3, f32[256,512]{1,0:T(8,128)} %get-tuple-element.37.base_ref), custom_call_target="tpu_custom_call" | custom-call | flops 1000 | bytes 1000 | tf_op jit(solution)/shard_map/pallas_call | solution.py:592
  (21 shorter events, 2.4 us)
Async XLA Ops:
  0.6 11.8 %copy-start.8 = (s32[2048]{0:T(1024)S(1)}, s32[2048]{0:T(1024)}, u32[]{:S(2)}) copy-start(s32[2048]{0:T(1024)} %param.29) | copy-start | bytes 24580
  0.6 12.5 %copy-start.7 = (s32[2048]{0:T(1024)S(1)}, s32[2048]{0:T(1024)}, u32[]{:S(2)}) copy-start(s32[2048]{0:T(1024)} %param.28) | copy-start | bytes 24580
  3.2 25.8 %all-to-all-start = ((bf16[32,32,512]{2,1,0:T(8,128)(2,1)}), bf16[32,32,512]{2,1,0:T(8,128)(2,1)S(1)}, u32[]{:S(2)}, u32[]{:S(2)}) async-start(bf16[32,32,512]{2,1,0:T(8,128)(2,1)} %bitcast.18), calls=%async_computation | async-start | bytes 2097152 | tf_op jit(solution)/shard_map/all_to_all | solution.py:436
  29.0 1.0 copy-start.2
  54.0 4.2 %collective-permute-start = (bf16[16,464,128]{2,1,0:T(8,128)(2,1)}, bf16[16,464,128]{2,1,0:T(8,128)(2,1)S(1)}, u32[]{:S(2)}, u32[]{:S(2)}) collective-permute-start(bf16[16,464,128]{2,1,0:T(8,128)(2,1)} %get-tuple-element.30), channel_id=1, source_target_pairs={{0,4},{4,0},{8,12},{12,8},{16,20},{20,16},{24,28},{28,24},{32,36},... | collective-permute-start | bytes 5701640 | tf_op jit(solution)/shard_map/ppermute | solution.py:545
  61.6 34.0 %all-to-all-start.1 = ((bf16[16,464,128]{2,1,0:T(8,128)(2,1)}), bf16[16,464,128]{2,1,0:T(8,128)(2,1)S(1)}, u32[]{:S(2)}, u32[]{:S(2)}) async-start(bf16[16,464,128]{2,1,0:T(8,128)(2,1)} %add_convert_fusion), calls=%async_computation.1 | async-start | bytes 3801088 | tf_op jit(solution)/shard_map/all_to_all | solution.py:548
  76.1 32.5 %copy-start.6 = (s32[32,32]{1,0:T(8,128)S(1)}, s32[32,32]{1,0:T(8,128)}, u32[]{:S(2)}) copy-start(s32[32,32]{1,0:T(8,128)} %rows_ref.1) | copy-start | bytes 12292
  95.6 4.8 %copy-start = (bf16[16,464,128]{2,1,0:T(8,128)(2,1)}, bf16[16,464,128]{2,1,0:T(8,128)(2,1)S(1)}, u32[]{:S(2)}) copy-start(bf16[16,464,128]{2,1,0:T(8,128)(2,1)S(1)} %all-to-all-done.1.parts_ref) | copy-start | bytes 5701636
  95.7 22.1 %all-to-all-start.2 = ((bf16[32,32,512]{2,1,0:T(8,128)(2,1)}), bf16[32,32,512]{2,1,0:T(8,128)(2,1)S(1)}, u32[]{:S(2)}, u32[]{:S(2)}) async-start(bf16[32,32,512]{2,1,0:T(8,128)(2,1)} %bitcast.24), calls=%async_computation.2 | async-start | bytes 2097152 | tf_op jit(solution)/shard_map/all_to_all | solution.py:579
  102.9 7.3 %collective-permute-start.1 = (bf16[464,128]{1,0:T(8,128)(2,1)}, bf16[464,128]{1,0:T(8,128)(2,1)S(1)}, u32[]{:S(2)}, u32[]{:S(2)}) collective-permute-start(bf16[464,128]{1,0:T(8,128)(2,1)} %get-tuple-element.41), channel_id=1, source_target_pairs={{0,1},{1,2},{2,3},{3,0},{4,5},{5,6},{6,7},{7,4},{8,9},{9,10},{10,1... | collective-permute-start | bytes 356360 | tf_op jit(solution)/shard_map/ppermute | solution.py:589
  104.6 9.1 %collective-permute-start.2 = (bf16[464,128]{1,0:T(8,128)(2,1)}, bf16[464,128]{1,0:T(8,128)(2,1)S(1)}, u32[]{:S(2)}, u32[]{:S(2)}) collective-permute-start(bf16[464,128]{1,0:T(8,128)(2,1)} %get-tuple-element.41), channel_id=1, source_target_pairs={{0,2},{1,3},{2,0},{3,1},{4,6},{5,7},{6,4},{7,5},{8,10},{9,11},{10,... | collective-permute-start | bytes 356360 | tf_op jit(solution)/shard_map/ppermute | solution.py:589
  107.9 5.8 %collective-permute-start.3 = (bf16[464,128]{1,0:T(8,128)(2,1)}, bf16[464,128]{1,0:T(8,128)(2,1)S(1)}, u32[]{:S(2)}, u32[]{:S(2)}) collective-permute-start(bf16[464,128]{1,0:T(8,128)(2,1)} %get-tuple-element.41), channel_id=1, source_target_pairs={{0,3},{1,0},{2,1},{3,2},{4,7},{5,4},{6,5},{7,6},{8,11},{9,8},{10,9... | collective-permute-start | bytes 356360 | tf_op jit(solution)/shard_map/ppermute | solution.py:589
  110.2 3.4 %copy-start.3 = (bf16[464,128]{1,0:T(8,128)(2,1)}, bf16[464,128]{1,0:T(8,128)(2,1)S(1)}, u32[]{:S(2)}) copy-start(bf16[464,128]{1,0:T(8,128)(2,1)S(1)} %collective-permute-done.1.refs_1_) | copy-start | bytes 356356
  113.7 0.6 copy-start.4
  113.7 0.7 copy-start.5
  117.7 1.0 copy-start.1
where the time goes:
time: 122 us
  Pallas kernels  52.7 us (43%)
  waiting for transfers between devices  36.3 us (30%)
  starting transfers between devices  23.2 us (19%)
  local copies, waits for them, and re-layouts  4.59 us (4%)
  other arithmetic  3.41 us (3%)
  between operations  1.38 us (1%)
    pallas_call x1, Pallas kernels, shards(): pl.pallas_call(main_kernel, in_specs=[smem, vmem, vmem, vmem] + [hbm] * 1...  24 us
    all_to_all x1, waiting for transfers between devices, shards(): lax.all_to_all(chip_sum, 'dom', split_axis=0, concat_axis=0, axis_index_g...  19.5 us
    all_to_all x1, starting transfers between devices, shards(): lax.all_to_all(outgoing.reshape(regions, cap, width), 'dom', split_axis=0...  8.59 us
    pallas_call x1, Pallas kernels, shards(): pl.pallas_call(before_kernel, grid=(n_chunks,), in_specs=[whole((n_chunks...  8.14 us
    all_to_all x1, waiting for transfers between devices, shards(): lax.all_to_all(outgoing.reshape(regions, cap, width), 'dom', split_axis=0...  7.14 us
    pallas_call x1, Pallas kernels, shards(): pl.pallas_call(senders_kernel, grid=(1,), in_specs=[vmem, vmem, one_block...  6.59 us
    ppermute x3, starting transfers between devices, shards(): lax.ppermute(total_bf16, 'rep', [(i, (i + k) % reps) for i in range(reps)])  5.66 us
    all_to_all x1, starting transfers between devices, shards(): lax.all_to_all(sent.reshape(regions, cap, width), 'dom', split_axis=0, co...  4.78 us
  transfers between devices with their start and end apart: 7, of which 6 were waited for; matrix products, arithmetic and copies ran while one was open for 2% of the time, Pallas kernels for 19%

commit v1 on v0

v1 whole, which is shorter than its diff:
```python
import jax
import jax.numpy as jnp
from jax import lax
from jax.experimental import pallas as pl
from jax.experimental.pallas import tpu as pltpu
from jax.sharding import PartitionSpec as P

epsilon = 1e-05
f32 = jnp.float32
bf16 = jnp.bfloat16
NT = (((1,), (1,)), ((), ()))
TN = (((0,), (0,)), ((), ()))
MAIN_LIMIT = 50
BEFORE_LIMIT = 60
CHUNK = 1024
PART = bf16
KEPT = bf16


def mm(a, b):
    return jnp.dot(a, b, preferred_element_type=f32)


def mm_nt(a, b):
    return lax.dot_general(a, b, NT, preferred_element_type=f32)


def mm_tn(a, b):
    return lax.dot_general(a, b, TN, preferred_element_type=f32)


def params(limit=16):
    return pltpu.CompilerParams(vmem_limit_bytes=limit * 1024 * 1024)


def cost(flops, moved):
    return pl.CostEstimate(flops=flops, bytes_accessed=moved, transcendentals=0)


def one_hot_t(row, first, count):
    ids = lax.broadcasted_iota(jnp.int32, (count, row.shape[1]), 0) + first
    return jnp.where(ids == row, 1.0, 0.0).astype(bf16)


def columns(row):
    k = row.shape[1]
    parts = [
        jnp.transpose(jnp.broadcast_to(row[:, i : i + 128], (128, 128))) for i in range(0, k, 128)
    ]
    return jnp.concatenate(parts, axis=0)


def one_hot(column, first, count):
    lane = lax.broadcasted_iota(jnp.int32, column.shape, 1)
    parts = [
        jnp.where(column == lane + (first + i), 1.0, 0.0).astype(bf16)
        for i in range(0, count, 128)
    ]
    return jnp.concatenate(parts, axis=1)


def sigmoid(value):
    return 0.5 * jnp.tanh(0.5 * value) + 0.5


def normalise(value, live=None):
    center = value - jnp.mean(value, axis=-1, keepdims=True)
    recip = lax.rsqrt(jnp.mean(center * center, axis=-1, keepdims=True) + epsilon)
    if live is not None:
        recip = jnp.where(live, recip, 0.0)
    return center * recip, recip


def norm_backward(upper, normed, recip):
    return recip * (
        upper
        - jnp.mean(upper, axis=-1, keepdims=True)
        - normed * jnp.mean(upper * normed, axis=-1, keepdims=True)
    )


def send_kernel(rows_ref, nodes_ref, out_hbm, out_ref, sems):
    n = nodes_ref.shape[0]
    regions, cap = rows_ref.shape
    listed = jnp.transpose(rows_ref[...])
    lane = lax.broadcasted_iota(jnp.int32, (cap, n), 1)
    pieces = sems.shape[0]
    group = regions // pieces
    copies = []
    for p in range(pieces):
        picks = jnp.concatenate(
            [
                jnp.where(listed[:, q : q + 1] == lane, 1.0, 0.0).astype(bf16)
                for q in range(p * group, (p + 1) * group)
            ],
            axis=0,
        )
        at = pl.ds(p * group * cap, group * cap)
        out_ref[at, :] = mm(picks, nodes_ref[...]).astype(bf16)
        copies.append(pltpu.make_async_copy(out_ref.at[at], out_hbm.at[at], sems.at[p]))
        copies[-1].start()
    for copy in copies:
        copy.wait()


def before_kernel(
    snd_ref,
    rcv_ref,
    edges_ref,
    nodes_ref,
    ein_ref,
    ebias_ref,
    part_ref,
    local_ref,
    far_ref,
    rcv_n_ref,
    table_scr,
):
    n, width = nodes_ref.shape
    remote = far_ref.shape[1]
    c = pl.program_id(0)

    @pl.when(c == 0)
    def _():
        table_scr[...] = mm(nodes_ref[...], ein_ref[2 * width :, :]).astype(bf16)

    snd = columns(snd_ref[pl.ds(c, 1), :])
    near = one_hot(columns(rcv_ref[pl.ds(c, 1), :]), 0, n)
    rcv_n_ref[...] = near
    local_ref[...] = mm(one_hot(snd, 0, n), nodes_ref[...]).astype(bf16)
    far_ref[...] = one_hot(snd, n, remote)
    part_ref[...] = (
        mm(edges_ref[...], ein_ref[:width, :]) + mm(near, table_scr[...]) + ebias_ref[...]
    ).astype(part_ref.dtype)


def deal(core, mats_ref, vecs, mine_ref, send_ref):
    blocks = mine_ref.shape[0]
    regions = 2 * blocks
    share, width = mats_ref.shape[0] // regions, mats_ref.shape[1]
    tail = jnp.concatenate(
        [vec[:, j : j + 128] for vec in vecs for j in range(0, width, 128)], axis=0
    ).astype(bf16)
    for out_ref, parity in ((mine_ref, core), (send_ref, 1 - core)):
        for i in range(blocks):
            at = pl.multiple_of((2 * i + parity) * share, 16)
            rows = mats_ref[pl.ds(at, share), :]
            for j in range(width // 128):
                out_ref[i, j * share : (j + 1) * share] = rows[:, j * 128 : (j + 1) * 128]
            out_ref[i, width // 128 * share :] = tail


def main_kernel(
    place_ref,
    live_ref,
    egain_ref,
    nbias_ref,
    ngain_ref,
    arrived_ref,
    part_hbm,
    local_hbm,
    far_hbm,
    rcv_n_hbm,
    cot_hbm,
    edges_hbm,
    nodes_hbm,
    ncot_hbm,
    ein_hbm,
    eout_hbm,
    nin_hbm,
    nout_hbm,
    hg_ref,
    base_ref,
    mine_ref,
    send_ref,
    part_ref,
    far_ref,
    x_ref,
    cot_ref,
    node_in_ref,
    ncot_ref,
    ws_ref,
    wr_ref,
    eout_ref,
    nin_ref,
    nout_ref,
    act_ref,
    slope_ref,
    normed_ref,
    recip_ref,
    mats_ref,
    pg_ref,
    chunk_sems,
    sems,
):
    count, width = part_ref.shape
    n = ncot_ref.shape[0]
    chunk = min(CHUNK, count)
    n_chunks = count // chunk
    streams = [
        (far_hbm, far_ref),
        (local_hbm, x_ref.at[:, pl.ds(width, width)]),
        (part_hbm, part_ref),
        (rcv_n_hbm, x_ref.at[:, pl.ds(2 * width, n)]),
        (cot_hbm, cot_ref),
        (edges_hbm, x_ref.at[:, pl.ds(0, width)]),
    ]

    def stream(k, c):
        src, dst = streams[k]
        at = pl.ds(c * chunk, chunk)
        return pltpu.make_async_copy(src.at[at], dst.at[at], chunk_sems.at[k, c])

    singles = [
        (ein_hbm.at[pl.ds(width, width)], ws_ref),
        (eout_hbm, eout_ref),
        (nodes_hbm, node_in_ref.at[:, pl.ds(0, width)]),
        (nin_hbm, nin_ref),
        (nout_hbm, nout_ref),
        (ncot_hbm, ncot_ref),
        (ein_hbm.at[pl.ds(2 * width, width)], wr_ref),
    ]
    single = [pltpu.make_async_copy(src, dst, sems.at[k]) for k, (src, dst) in enumerate(singles)]
    stream(0, 0).start()
    stream(1, 0).start()
    single[0].start()
    stream(2, 0).start()
    single[1].start()
    for c in range(1, n_chunks):
        for k in range(3):
            stream(k, c).start()
    for c in range(n_chunks):
        stream(3, c).start()
    for k in range(2, 6):
        single[k].start()
    for c in range(n_chunks):
        for k in range(4, 6):
            stream(k, c).start()
    single[6].start()

    egain = egain_ref[...]

    def rows_at(c):
        return pl.ds(c * chunk, chunk)

    def pick(c):
        here = rows_at(c)
        x_ref[here, width : 2 * width] += mm(far_ref[here, :], arrived_ref[...]).astype(bf16)

    def activate(c):
        here = rows_at(c)
        hidden = part_ref[here, :] + mm(x_ref[here, width : 2 * width], ws_ref[...])
        s = sigmoid(hidden)
        act_ref[here, :] = (hidden * s).astype(bf16)
        slope_ref[here, :] = (s * (1.0 + hidden * (1.0 - s))).astype(KEPT)

    def send_message(c):
        here = rows_at(c)
        live = lax.broadcasted_iota(jnp.int32, (chunk, 1), 0) + c * chunk < live_ref[0]
        normed, recip = normalise(mm(act_ref[here, :], eout_ref[...]), live)
        normed_ref[here, :] = normed.astype(KEPT)
        recip_ref[here, :] = recip
        pg_ref[here, :] = (normed * egain).astype(bf16)

    def skewed(stages, before):
        for t in range(n_chunks + len(stages) - 1):
            for k in range(len(stages)):
                if 0 <= t - k < n_chunks:
                    before[k](t - k)
            for k in reversed(range(len(stages))):
                if 0 <= t - k < n_chunks:
                    stages[k](t - k)

    def nothing(c):
        pass

    def wait_pick(c):
        stream(0, c).wait()
        stream(1, c).wait()

    def wait_activate(c):
        stream(2, c).wait()
        if c == 0:
            single[0].wait()

    def wait_message(c):
        if c == 0:
            single[1].wait()

    skewed([pick, activate, send_message], [wait_pick, wait_activate, wait_message])
    for c in range(n_chunks):
        stream(3, c).wait()
    agg = mm_tn(x_ref[:, 2 * width :], pg_ref[...])

    for k in range(2, 6):
        single[k].wait()
    node_in_ref[:, width:] = agg.astype(bf16)
    node_in = node_in_ref[...]
    nodes = node_in_ref[:, :width]
    hidden = mm(node_in, nin_ref[...]) + nbias_ref[...]
    s = sigmoid(hidden)
    act = (hidden * s).astype(bf16)
    normed, recip = normalise(mm(act, nout_ref[...]))
    upstream = ncot_ref[...].astype(f32)
    pre_grad = norm_backward(upstream * ngain_ref[...], normed, recip).astype(bf16)
    hidden_grad = (mm_nt(pre_grad, nout_ref[...]) * (s * (1.0 + hidden * (1.0 - s)))).astype(bf16)
    node_in_grad = mm_nt(hidden_grad, nin_ref[...])
    agg_grad = node_in_grad[:, width:].astype(bf16)
    vecs = [
        None,
        None,
        jnp.sum(hidden_grad.astype(f32), axis=0, keepdims=True),
        jnp.sum(upstream * normed, axis=0, keepdims=True),
    ]

    def take_gradient(c):
        here = rows_at(c)
        message_grad = cot_ref[here, :].astype(f32) + mm(x_ref[here, 2 * width :], agg_grad)
        edge_normed = normed_ref[here, :].astype(f32)
        term = jnp.sum(message_grad * edge_normed, axis=0, keepdims=True)
        vecs[1] = term if c == 0 else vecs[1] + term
        pg_ref[here, :] = norm_backward(
            message_grad * egain, edge_normed, recip_ref[here, :]
        ).astype(bf16)

    def pass_gradient(c):
        here = rows_at(c)
        edge_grad = (mm_nt(pg_ref[here, :], eout_ref[...]) * slope_ref[here, :].astype(f32)).astype(bf16)
        hg_ref[here, :] = edge_grad
        term = jnp.sum(edge_grad.astype(f32), axis=0, keepdims=True)
        vecs[0] = term if c == 0 else vecs[0] + term

    def wait_take(c):
        stream(4, c).wait()

    skewed([take_gradient, pass_gradient], [wait_take, nothing])
    for c in range(n_chunks):
        stream(5, c).wait()
    by_inputs = mm_tn(x_ref[...], hg_ref[...])

    single[6].wait()
    received = by_inputs[2 * width :].astype(bf16)
    base_ref[...] = (
        upstream + node_in_grad[:, :width] + mm_nt(received, wr_ref[...])
    )
    mats_ref[: 2 * width, :] = by_inputs[: 2 * width].astype(bf16)
    mats_ref[2 * width : 3 * width, :] = mm_tn(nodes, received).astype(bf16)
    mats_ref[3 * width : 4 * width, :] = mm_tn(act_ref[...], pg_ref[...]).astype(bf16)
    mats_ref[4 * width : 6 * width, :] = mm_tn(node_in, hidden_grad).astype(bf16)
    mats_ref[6 * width :, :] = mm_tn(act, pre_grad).astype(bf16)
    deal(place_ref[0], mats_ref, vecs, mine_ref, send_ref)


def senders_kernel(snd_ref, hg_ref, ws_ref, base_ref, sent_ref, out_ref):
    n, width = base_ref.shape
    remote = sent_ref.shape[0]
    snd = snd_ref[...]
    local = mm(one_hot_t(snd, 0, n), hg_ref[...]).astype(bf16)
    out_ref[...] = base_ref[...] + mm_nt(local, ws_ref[...])
    tile = 256 if remote % 256 == 0 else remote

    @pl.loop(0, remote // tile)
    def _(i):
        at = pl.multiple_of(i * tile, tile)
        part = mm(one_hot_t(snd, n + at, tile), hg_ref[...]).astype(bf16)
        sent_ref[pl.ds(at, tile), :] = part


def edges_kernel(hg_ref, cot_ref, w_ref, out_ref):
    out_ref[...] = (cot_ref[...].astype(f32) + mm_nt(hg_ref[...], w_ref[...])).astype(bf16)


def finish_kernel(rows_ref, returned_ref, ws_ref, base_ref, out_ref):
    n, width = base_ref.shape
    own = mm(one_hot_t(rows_ref[...], 0, n), returned_ref[...]).astype(bf16)
    out_ref[...] = (base_ref[...] + mm_nt(own, ws_ref[...])).astype(bf16)


def over_chips_kernel(parts_ref, own_ref, sent_ref):
    total = jnp.sum(parts_ref[...].astype(f32), axis=0)
    own_ref[...] = total
    sent_ref[...] = total.astype(bf16)


def join_kernel(*refs):
    mats_ref, vecs_ref = refs[-2:]
    share, width = mats_ref.shape
    total = refs[0][...]
    for ref in refs[1:-2]:
        total = total + ref[...].astype(f32)
    slabs = width // 128
    for j in range(slabs):
        mats_ref[:, j * 128 : (j + 1) * 128] = total[j * share : (j + 1) * share]
        for k in range(4):
            at = slabs * share + k * slabs + j
            vecs_ref[k : k + 1, j * 128 : (j + 1) * 128] = total[at : at + 1]


def shards(
    node_feat,
    edge_feat,
    node_cot,
    edge_cot,
    edge_in_w,
    edge_bias,
    edge_out_w,
    edge_gain,
    node_in_w,
    node_bias,
    node_out_w,
    node_gain,
    senders,
    receivers,
    send_rows,
    live_edges,
):
    nodes = node_feat[0]
    edges = edge_feat[0]
    cots = edge_cot[0]
    n, width = nodes.shape
    count = edges.shape[0]
    regions, cap = send_rows.shape
    remote = regions * cap
    chunk = min(CHUNK, count)
    n_chunks = count // chunk
    rows = edge_in_w.shape[0] + edge_out_w.shape[0] + node_in_w.shape[0] + node_out_w.shape[0]
    share = rows // regions
    chips = regions // 2
    reps = lax.axis_size("rep")
    core = lax.rem(lax.axis_index("dom"), 2).reshape(1)
    smem = pl.BlockSpec(memory_space=pltpu.SMEM)
    vmem = pl.BlockSpec(memory_space=pltpu.VMEM)
    hbm = pl.BlockSpec(memory_space=pl.ANY)
    shape = jax.ShapeDtypeStruct

    def whole(shape):
        return pl.BlockSpec(shape, lambda i: (0,) * len(shape))

    def rows_of(width):
        return pl.BlockSpec((chunk, width), lambda i: (i, 0))

    outgoing = pl.pallas_call(
        send_kernel,
        out_specs=hbm,
        out_shape=shape((remote, width), bf16),
        scratch_shapes=[
            pltpu.VMEM((remote, width), bf16),
            pltpu.SemaphoreType.DMA((4,)),
        ],
        compiler_params=params(58),
        cost_estimate=cost(2 * remote * n * width, 4 * remote * width),
    )(send_rows, nodes)
    arrived = lax.all_to_all(
        outgoing.reshape(regions, cap, width), "dom", split_axis=0, concat_axis=0, tiled=True
    ).reshape(remote, width)

    hidden_part, local, far, rcv_n = pl.pallas_call(
        before_kernel,
        grid=(n_chunks,),
        in_specs=[
            whole((n_chunks, chunk)),
            whole((n_chunks, chunk)),
            rows_of(width),
            whole((n, width)),
            whole(edge_in_w.shape),
            whole((1, width)),
        ],
        out_specs=[
            rows_of(width),
            rows_of(width),
            rows_of(remote),
            rows_of(n),
        ],
        out_shape=[
            shape((count, width), PART),
            shape((count, width), bf16),
            shape((count, remote), bf16),
            shape((count, n), bf16),
        ],
        scratch_shapes=[pltpu.VMEM((n, width), bf16)],
        compiler_params=params(BEFORE_LIMIT),
        cost_estimate=cost(6_000_000_000, 16_000_000),
    )(
        senders.reshape(n_chunks, chunk),
        receivers.reshape(n_chunks, chunk),
        edges,
        nodes,
        edge_in_w,
        edge_bias.reshape(1, width),
    )

    slab = (share * width + 4 * width) // 128
    dealt = (chips, slab, 128)
    hidden_grad, base, mine, to_other = pl.pallas_call(
        main_kernel,
        in_specs=[smem] * 2 + [vmem] * 4 + [hbm] * 12,
        out_specs=[vmem] * 4,
        out_shape=[
            shape((count, width), bf16),
            shape((n, width), f32),
            shape(dealt, bf16),
            shape(dealt, bf16),
        ],
        scratch_shapes=[
            pltpu.VMEM((count, width), PART),
            pltpu.VMEM((count, remote), bf16),
            pltpu.VMEM((count, 2 * width + n), bf16),
            pltpu.VMEM((count, width), bf16),
            pltpu.VMEM((n, 2 * width), bf16),
            pltpu.VMEM((n, width), bf16),
            pltpu.VMEM((width, width), bf16),
            pltpu.VMEM((width, width), bf16),
            pltpu.VMEM(edge_out_w.shape, bf16),
            pltpu.VMEM(node_in_w.shape, bf16),
            pltpu.VMEM(node_out_w.shape, bf16),
            pltpu.VMEM((count, width), bf16),
            pltpu.VMEM((count, width), KEPT),
            pltpu.VMEM((count, width), KEPT),
            pltpu.VMEM((count, 1), f32),
            pltpu.VMEM((rows, width), bf16),
            pltpu.VMEM((count, width), bf16),
            pltpu.SemaphoreType.DMA((6, n_chunks)),
            pltpu.SemaphoreType.DMA((7,)),
        ],
        compiler_params=params(MAIN_LIMIT),
        cost_estimate=cost(16_000_000_000, 30_000_000),
    )(
        core,
        live_edges,
        edge_gain.reshape(1, width),
        node_bias.reshape(1, width),
        node_gain.reshape(1, width),
        arrived,
        hidden_part,
        local,
        far,
        rcv_n,
        cots,
        edges,
        nodes,
        node_cot[0],
        edge_in_w,
        edge_out_w,
        node_in_w,
        node_out_w,
    )

    w_s = edge_in_w[width : 2 * width]
    from_other = lax.ppermute(to_other, "dom", [(i, i ^ 1) for i in range(regions)])
    chip_sum = (mine.astype(f32) + from_other.astype(f32)).astype(bf16)
    chip_sum, hidden_grad = lax.optimization_barrier((chip_sum, hidden_grad))
    by_chip = lax.all_to_all(
        chip_sum,
        "dom",
        split_axis=0,
        concat_axis=0,
        axis_index_groups=[list(range(c, regions, 2)) for c in range(2)],
        tiled=True,
    )
    sent, base = pl.pallas_call(
        senders_kernel,
        out_shape=(shape((remote, width), bf16), shape((n, width), f32)),
        compiler_params=params(),
        cost_estimate=cost(1000, 1000),
    )(senders.reshape(1, count), hidden_grad, w_s, base)
    grad_edges = pl.pallas_call(
        edges_kernel,
        grid=(n_chunks,),
        in_specs=[
            rows_of(width),
            rows_of(width),
            pl.BlockSpec((width, width), lambda i: (0, 0)),
        ],
        out_specs=rows_of(width),
        out_shape=shape((count, width), bf16),
        compiler_params=params(),
        cost_estimate=cost(1000, 1000),
    )(hidden_grad, cots, edge_in_w)

    by_chip, sent, grad_edges = lax.optimization_barrier((by_chip, sent, grad_edges))
    returned = lax.all_to_all(
        sent.reshape(regions, cap, width), "dom", split_axis=0, concat_axis=0, tiled=True
    ).reshape(remote, width)
    total, total_bf16 = pl.pallas_call(
        over_chips_kernel,
        out_shape=(shape((slab, 128), f32), shape((slab, 128), bf16)),
        compiler_params=params(),
        cost_estimate=cost(1_000_000, 2_000_000),
    )(by_chip)
    totals = [total] + [
        lax.ppermute(total_bf16, "rep", [(i, (i + k) % reps) for i in range(reps)])
        for k in range(1, reps)
    ]
    grad_nodes = pl.pallas_call(
        finish_kernel,
        out_shape=shape((n, width), bf16),
        compiler_params=params(),
        cost_estimate=cost(1000, 1000),
    )(send_rows.reshape(1, remote), returned, w_s, base)
    own_rows, vector_total = pl.pallas_call(
        join_kernel,
        out_shape=(shape((share, width), f32), shape((4, width), f32)),
        compiler_params=params(),
    )(*totals)
    return (grad_nodes[None], grad_edges[None], own_rows, vector_total)


def solution(mesh):
    in_specs = (
        P("rep", "dom", None),
        P("rep", "dom", None),
        P("rep", "dom", None),
        P("rep", "dom", None),
        P(),
        P(),
        P(),
        P(),
        P(),
        P(),
        P(),
        P(),
        P("dom"),
        P("dom"),
        P("dom", None),
        P("dom"),
    )
    out_specs = (P("rep", "dom", None), P("rep", "dom", None), P("dom", None), P())
    return jax.shard_map(shards, mesh=mesh, in_specs=in_specs, out_specs=out_specs, check_vma=False)
```

time: 122 us -> 117 us (0.959)
  Pallas kernels: 52.7 us -> 41.8 us
  waiting for transfers between devices: 36.3 us -> 39.5 us
  local copies, waits for them, and re-layouts: 4.59 us -> 6.4 us
    pallas_call x4, Pallas kernels: 36.1 us -> 29.4 us  [the longest x1 21.9 us: shards(): pl.pallas_call(main_kernel, in_specs=[smem] * 2 + [vmem] * 4 + [hbm] * 12...]
    all_to_all x1, waiting for transfers between devices: 1.5 us -> 4.21 us  [shards(): lax.all_to_all(sent.reshape(regions, cap, width), 'dom', split_axis=0, co...]
    pallas_call x1, Pallas kernels: 4.16 us -> 2.46 us  [shards(): pl.pallas_call(edges_kernel, grid=(n_chunks,), in_specs=[rows_of(width),...]
    unnamed x18 -> x32, local copies, waits for them, and re-layouts: 2.7 us -> 4.03 us
  transfers between devices with their start and end apart: 7 -> 7, of which waited for: 6 -> 6; matrix products, arithmetic and copies ran while one was open for 2% -> 2% of each run, Pallas kernels for 19% -> 14%
where the time goes in v1:
time: 117 us
  Pallas kernels  41.8 us (36%)
  waiting for transfers between devices  39.5 us (34%)
  starting transfers between devices  24.1 us (21%)
  local copies, waits for them, and re-layouts  6.4 us (5%)
  other arithmetic  3.31 us (3%)
  between operations  1.5 us (1%)
    pallas_call x1, Pallas kernels, shards(): pl.pallas_call(main_kernel, in_specs=[smem] * 2 + [vmem] * 4 + [hbm] * 12...  21.9 us
    all_to_all x1, waiting for transfers between devices, shards(): lax.all_to_all(chip_sum, 'dom', split_axis=0, concat_axis=0, axis_index_g...  19.1 us
    all_to_all x1, starting transfers between devices, shards(): lax.all_to_all(outgoing.reshape(regions, cap, width), 'dom', split_axis=0...  8.6 us
    all_to_all x1, waiting for transfers between devices, shards(): lax.all_to_all(outgoing.reshape(regions, cap, width), 'dom', split_axis=0...  7.81 us
    pallas_call x1, Pallas kernels, shards(): pl.pallas_call(before_kernel, grid=(n_chunks,), in_specs=[whole((n_chunks...  7.39 us
    ppermute x3, starting transfers between devices, shards(): lax.ppermute(total_bf16, 'rep', [(i, (i + k) % reps) for i in range(reps)])  5.73 us
    all_to_all x1, starting transfers between devices, shards(): lax.all_to_all(sent.reshape(regions, cap, width), 'dom', split_axis=0, co...  4.78 us
    ppermute x3, waiting for transfers between devices, shards(): lax.ppermute(total_bf16, 'rep', [(i, (i + k) % reps) for i in range(reps)])  4.73 us
  transfers between devices with their start and end apart: 7, of which 6 were waited for; matrix products, arithmetic and copies ran while one was open for 2% of the time, Pallas kernels for 14%

profile of v1, /device:TPU:1, one launch (start us, length us, event | category | flops | bytes accessed | tf_op | source)
XLA Modules:
  0.0 116.6 jit_solution(5334304575678769892)
XLA Ops:
  0.7 2.4 %shard_map.183 = bf16[1024,512]{1,0:T(8,128)(2,1)} custom-call(s32[32,32]{1,0:T(8,128)} %rows_ref.1, bf16[256,512]{1,0:T(8,128)(2,1)} %bitcast.21), custom_call_target="tpu_custom_call" | custom-call | flops 268435456 | bytes 2097152 | tf_op jit(solution)/shard_map/pallas_call | solution.py:442
  3.0 8.6 %all-to-all-start = ((bf16[32,32,512]{2,1,0:T(8,128)(2,1)}), bf16[32,32,512]{2,1,0:T(8,128)(2,1)S(1)}, u32[]{:S(2)}, u32[]{:S(2)}) async-start(bf16[32,32,512]{2,1,0:T(8,128)(2,1)} %bitcast.29), calls=%async_computation | async-start | bytes 2097152 | tf_op jit(solution)/shard_map/all_to_all | solution.py:453
  13.6 7.4 %shard_map.184 = (bf16[2048,512]{1,0:T(8,128)(2,1)}, bf16[2048,512]{1,0:T(8,128)(2,1)}, bf16[2048,1024]{1,0:T(8,128)(2,1)}, bf16[2048,256]{1,0:T(8,128)(2,1)}) custom-call(s32[2,1024]{1,0:T(2,128)} %reshape.54.snd_ref, s32[2,1024]{1,0:T(2,128)} %reshape.55.rcv_ref, bf16[2048,512]{1,0:T(8,128)(2,1)} %bitcast.32, bf16[256,512]{1,0:T(8,128)(2,1)} %bitcast.22, ...), custom_call_target="tpu_custom_call" | custom-call | flops 6000000000 | bytes 16000000 | tf_op jit(solution)/shard_map/pallas_call | solution.py:457
  21.0 7.8 %all-to-all-done = bf16[32,32,512]{2,1,0:T(8,128)(2,1)S(1)} async-done(((bf16[32,32,512]{2,1,0:T(8,128)(2,1)}), bf16[32,32,512]{2,1,0:T(8,128)(2,1)S(1)}, u32[]{:S(2)}, u32[]{:S(2)}) %all-to-all-start) | async-done | bytes 1048608 | tf_op jit(solution)/shard_map/all_to_all | solution.py:453
  28.9 21.9 %shard_map.185 = (bf16[2048,512]{1,0:T(8,128)(2,1)}, f32[256,512]{1,0:T(8,128)S(1)}, bf16[16,464,128]{2,1,0:T(8,128)(2,1)}, bf16[16,464,128]{2,1,0:T(8,128)(2,1)}) custom-call(s32[1]{0:T(128)} %bitcast.place_ref, s32[1]{0:T(128)S(6)} %copy.20.live_ref, f32[1,512]{1,0:T(1,128)S(1)} %bitcast.26, f32[1,512]{1,0:T(1,128)S(1)} %bitcast.27, ...), custom_call_target="tpu_custom_call" | custom-call | flops 16000000000 | bytes 30000000 | tf_op jit(solution)/shard_map/pallas_call | solution.py:494
  51.3 3.7 %collective-permute-done = bf16[16,464,128]{2,1,0:T(8,128)(2,1)S(1)} collective-permute-done((bf16[16,464,128]{2,1,0:T(8,128)(2,1)}, bf16[16,464,128]{2,1,0:T(8,128)(2,1)S(1)}, u32[]{:S(2)}, u32[]{:S(2)}) %collective-permute-start) | collective-permute-done | bytes 1900576 | tf_op jit(solution)/shard_map/ppermute | solution.py:549
  55.0 3.3 %add_convert_fusion = bf16[16,464,128]{2,1,0:T(8,128)(2,1)} fusion(bf16[16,464,128]{2,1,0:T(8,128)(2,1)S(1)} %collective-permute-done, bf16[16,464,128]{2,1,0:T(8,128)(2,1)} %get-tuple-element.27), kind=kLoop, calls=%fused_computation | loop fusion | flops 3801088 | bytes 5701632 | tf_op jit(solution)/shard_map/convert_element_type | solution.py:550
  58.3 4.6 %all-to-all-start.1 = ((bf16[16,464,128]{2,1,0:T(8,128)(2,1)}), bf16[16,464,128]{2,1,0:T(8,128)(2,1)}, u32[]{:S(2)}, u32[]{:S(2)}) async-start(bf16[16,464,128]{2,1,0:T(8,128)(2,1)} %add_convert_fusion), calls=%async_computation.1 | async-start | bytes 3801088 | tf_op jit(solution)/shard_map/all_to_all | solution.py:552
  62.9 1.1 slice.3.ws_ref
  64.0 1.4 %copy-done.1 = bf16[1536,512]{1,0:T(8,128)(2,1)S(1)} copy-done((bf16[1536,512]{1,0:T(8,128)(2,1)S(1)}, bf16[1536,512]{1,0:T(8,128)(2,1)}, u32[]{:S(2)}) %copy-start.1) | copy-done | bytes 1572888
  65.4 1.6 %copy-done.2 = bf16[1,2048,512]{2,1,0:T(8,128)(2,1)S(1)} copy-done((bf16[1,2048,512]{2,1,0:T(8,128)(2,1)S(1)}, bf16[1,2048,512]{2,1,0:T(8,128)(2,1)}, u32[]{:S(2)}) %copy-start.2) | copy-done | bytes 2097176
  67.0 2.5 %shard_map.187 = bf16[2048,512]{1,0:T(8,128)(2,1)} custom-call(bf16[2048,512]{1,0:T(8,128)(2,1)S(1)} %copy-done, bf16[2048,512]{1,0:T(8,128)(2,1)S(1)} %bitcast.18, bf16[1536,512]{1,0:T(8,128)(2,1)S(1)} %copy-done.1), custom_call_target="tpu_custom_call" | custom-call | flops 1000 | bytes 1000 | tf_op jit(solution)/shard_map/pallas_call | solution.py:566
  69.4 3.7 %shard_map.186 = (bf16[1024,512]{1,0:T(8,128)(2,1)S(1)}, f32[256,512]{1,0:T(8,128)S(1)}) custom-call(s32[1,2048]{1,0:T(1,128)S(1)} %bitcast.24, bf16[2048,512]{1,0:T(8,128)(2,1)S(1)} %copy-done, bf16[512,512]{1,0:T(8,128)(2,1)S(1)} %slice.3.ws_ref, f32[256,512]{1,0:T(8,128)S(1)} %copy-done.5), custom_call_target="tpu_custom_call" | custom-call | flops 1000 | bytes 1000 | tf_op jit(solution)/shard_map/pallas_call | solution.py:560
  73.2 1.0 copy-done.3
  74.2 19.1 %all-to-all-done.1.parts_ref = bf16[16,464,128]{2,1,0:T(8,128)(2,1)} async-done(((bf16[16,464,128]{2,1,0:T(8,128)(2,1)}), bf16[16,464,128]{2,1,0:T(8,128)(2,1)}, u32[]{:S(2)}, u32[]{:S(2)}) %all-to-all-start.1) | async-done | bytes 1900576 | tf_op jit(solution)/shard_map/all_to_all | solution.py:552
  93.2 4.8 %all-to-all-start.2 = ((bf16[32,32,512]{2,1,0:T(8,128)(2,1)}), bf16[32,32,512]{2,1,0:T(8,128)(2,1)S(1)}, u32[]{:S(2)}, u32[]{:S(2)}) async-start(bf16[32,32,512]{2,1,0:T(8,128)(2,1)} %bitcast.19), calls=%async_computation.2 | async-start | bytes 2097152 | tf_op jit(solution)/shard_map/all_to_all | solution.py:581
  98.0 1.8 %shard_map.189 = (f32[464,128]{1,0:T(8,128)S(1)}, bf16[464,128]{1,0:T(8,128)(2,1)S(1)}) custom-call(bf16[16,464,128]{2,1,0:T(8,128)(2,1)} %all-to-all-done.1.parts_ref), custom_call_target="tpu_custom_call" | custom-call | flops 1000000 | bytes 2000000 | tf_op jit(solution)/shard_map/pallas_call | solution.py:584
  99.8 1.7 %collective-permute-start.1 = (bf16[464,128]{1,0:T(8,128)(2,1)S(1)}, bf16[464,128]{1,0:T(8,128)(2,1)S(1)}, u32[]{:S(2)}, u32[]{:S(2)}) collective-permute-start(bf16[464,128]{1,0:T(8,128)(2,1)S(1)} %get-tuple-element.39), channel_id=1, source_target_pairs={{0,1},{1,2},{2,3},{3,0},{4,5},{5,6},{6,7},{7,4},{8,9},{9,10},{10,1... | collective-permute-start | bytes 356360 | tf_op jit(solution)/shard_map/ppermute | solution.py:591
  101.5 3.3 %collective-permute-start.2 = (bf16[464,128]{1,0:T(8,128)(2,1)S(1)}, bf16[464,128]{1,0:T(8,128)(2,1)S(1)}, u32[]{:S(2)}, u32[]{:S(2)}) collective-permute-start(bf16[464,128]{1,0:T(8,128)(2,1)S(1)} %get-tuple-element.39), channel_id=1, source_target_pairs={{0,2},{1,3},{2,0},{3,1},{4,6},{5,7},{6,4},{7,5},{8,10},{9,11},{10,... | collective-permute-start | bytes 356360 | tf_op jit(solution)/shard_map/ppermute | solution.py:591
  105.6 1.3 %collective-permute-done.1.refs_1_ = bf16[464,128]{1,0:T(8,128)(2,1)S(1)} collective-permute-done((bf16[464,128]{1,0:T(8,128)(2,1)S(1)}, bf16[464,128]{1,0:T(8,128)(2,1)S(1)}, u32[]{:S(2)}, u32[]{:S(2)}) %collective-permute-start.1) | collective-permute-done | bytes 118816 | tf_op jit(solution)/shard_map/ppermute | solution.py:591
  106.9 3.4 %collective-permute-done.2.refs_2_ = bf16[464,128]{1,0:T(8,128)(2,1)S(1)} collective-permute-done((bf16[464,128]{1,0:T(8,128)(2,1)S(1)}, bf16[464,128]{1,0:T(8,128)(2,1)S(1)}, u32[]{:S(2)}, u32[]{:S(2)}) %collective-permute-start.2) | collective-permute-done | bytes 118816 | tf_op jit(solution)/shard_map/ppermute | solution.py:591
  110.3 0.8 shard_map.190
  111.1 4.2 %all-to-all-done.2 = bf16[32,32,512]{2,1,0:T(8,128)(2,1)S(1)} async-done(((bf16[32,32,512]{2,1,0:T(8,128)(2,1)}), bf16[32,32,512]{2,1,0:T(8,128)(2,1)S(1)}, u32[]{:S(2)}, u32[]{:S(2)}) %all-to-all-start.2) | async-done | bytes 1048608 | tf_op jit(solution)/shard_map/all_to_all | solution.py:581
  115.3 1.4 %shard_map.188 = bf16[256,512]{1,0:T(8,128)(2,1)} custom-call(s32[1,1024]{1,0:T(1,128)S(1)} %reshape.47.rows_ref, bf16[1024,512]{1,0:T(8,128)(2,1)S(1)} %bitcast.16, bf16[512,512]{1,0:T(8,128)(2,1)S(1)} %slice.3.ws_ref, f32[256,512]{1,0:T(8,128)S(1)} %get-tuple-element.35.base_ref), custom_call_target="tpu_custom_call" | custom-call | flops 1000 | bytes 1000 | tf_op jit(solution)/shard_map/pallas_call | solution.py:594
  (35 shorter events, 2.6 us)
Async XLA Ops:
  0.6 11.0 %copy-start.7 = (s32[2048]{0:T(1024)S(1)}, s32[2048]{0:T(1024)}, u32[]{:S(2)}) copy-start(s32[2048]{0:T(1024)} %param.28) | copy-start | bytes 24580
  0.6 11.6 %copy-start.15 = (s32[2048]{0:T(1024)S(1)}, s32[2048]{0:T(1024)}, u32[]{:S(2)}) copy-start(s32[2048]{0:T(1024)} %param.29) | copy-start | bytes 24580
  3.0 25.8 %all-to-all-start = ((bf16[32,32,512]{2,1,0:T(8,128)(2,1)}), bf16[32,32,512]{2,1,0:T(8,128)(2,1)S(1)}, u32[]{:S(2)}, u32[]{:S(2)}) async-start(bf16[32,32,512]{2,1,0:T(8,128)(2,1)} %bitcast.29), calls=%async_computation | async-start | bytes 2097152 | tf_op jit(solution)/shard_map/all_to_all | solution.py:453
  13.5 15.3 %copy-start.6 = (bf16[1,256,512]{2,1,0:T(8,128)(2,1)S(1)}, bf16[1,256,512]{2,1,0:T(8,128)(2,1)}, u32[]{:S(2)}) copy-start(bf16[1,256,512]{2,1,0:T(8,128)(2,1)} %param.16) | copy-start | bytes 786436
  13.5 15.3 %copy-start.8 = (bf16[512,512]{1,0:T(8,128)(2,1)S(1)}, bf16[512,512]{1,0:T(8,128)(2,1)}, u32[]{:S(2)}) copy-start(bf16[512,512]{1,0:T(8,128)(2,1)} %eout_hbm.1) | copy-start | bytes 1572868
  13.5 15.3 %copy-start.9 = (bf16[512,512]{1,0:T(8,128)(2,1)S(1)}, bf16[512,512]{1,0:T(8,128)(2,1)}, u32[]{:S(2)}) copy-start(bf16[512,512]{1,0:T(8,128)(2,1)} %nout_hbm.1) | copy-start | bytes 1572868
  13.6 15.3 %copy-start.10 = (bf16[1,256,512]{2,1,0:T(8,128)(2,1)S(1)}, bf16[1,256,512]{2,1,0:T(8,128)(2,1)}, u32[]{:S(2)}) copy-start(bf16[1,256,512]{2,1,0:T(8,128)(2,1)} %param.18) | copy-start | bytes 786436
  13.6 15.3 %copy-start.11 = (f32[512]{0:T(512)S(1)}, f32[512]{0:T(512)}, u32[]{:S(2)}) copy-start(f32[512]{0:T(512)} %param.23) | copy-start | bytes 6148
  13.6 15.3 %copy-start.12 = (f32[512]{0:T(512)S(1)}, f32[512]{0:T(512)}, u32[]{:S(2)}) copy-start(f32[512]{0:T(512)} %param.25) | copy-start | bytes 6148
  13.6 15.3 %copy-start.13 = (f32[512]{0:T(512)S(1)}, f32[512]{0:T(512)}, u32[]{:S(2)}) copy-start(f32[512]{0:T(512)} %param.27) | copy-start | bytes 6148
  50.8 7.5 %copy-start.4 = (f32[256,512]{1,0:T(8,128)}, f32[256,512]{1,0:T(8,128)S(1)}, u32[]{:S(2)}) copy-start(f32[256,512]{1,0:T(8,128)S(1)} %get-tuple-element.32.base_ref) | copy-start | bytes 1572868
  50.8 4.2 %collective-permute-start = (bf16[16,464,128]{2,1,0:T(8,128)(2,1)}, bf16[16,464,128]{2,1,0:T(8,128)(2,1)S(1)}, u32[]{:S(2)}, u32[]{:S(2)}) collective-permute-start(bf16[16,464,128]{2,1,0:T(8,128)(2,1)} %get-tuple-element.28), channel_id=1, source_target_pairs={{0,4},{4,0},{8,12},{12,8},{16,20},{20,16},{24,28},{28,24},{32,36},... | collective-permute-start | bytes 5701640 | tf_op jit(solution)/shard_map/ppermute | solution.py:549
  58.3 5.7 %copy-start = (bf16[2048,512]{1,0:T(8,128)(2,1)S(1)}, bf16[2048,512]{1,0:T(8,128)(2,1)}, u32[]{:S(2)}) copy-start(bf16[2048,512]{1,0:T(8,128)(2,1)} %get-tuple-element.31.hg_ref) | copy-start | bytes 6291460
  58.3 34.9 %all-to-all-start.1 = ((bf16[16,464,128]{2,1,0:T(8,128)(2,1)}), bf16[16,464,128]{2,1,0:T(8,128)(2,1)}, u32[]{:S(2)}, u32[]{:S(2)}) async-start(bf16[16,464,128]{2,1,0:T(8,128)(2,1)} %add_convert_fusion), calls=%async_computation.1 | async-start | bytes 3801088 | tf_op jit(solution)/shard_map/all_to_all | solution.py:552
  64.0 1.4 %copy-start.1 = (bf16[1536,512]{1,0:T(8,128)(2,1)S(1)}, bf16[1536,512]{1,0:T(8,128)(2,1)}, u32[]{:S(2)}) copy-start(bf16[1536,512]{1,0:T(8,128)(2,1)} %w_ref.1) | copy-start | bytes 4718596
  65.4 1.6 %copy-start.2 = (bf16[1,2048,512]{2,1,0:T(8,128)(2,1)S(1)}, bf16[1,2048,512]{2,1,0:T(8,128)(2,1)}, u32[]{:S(2)}) copy-start(bf16[1,2048,512]{2,1,0:T(8,128)(2,1)} %param.19) | copy-start | bytes 6291460
  67.0 2.5 %copy-start.5 = (f32[256,512]{1,0:T(8,128)S(1)}, f32[256,512]{1,0:T(8,128)}, u32[]{:S(2)}) copy-start(f32[256,512]{1,0:T(8,128)} %copy-done.4) | copy-start | bytes 1572868
  73.2 1.0 copy-start.3
  74.1 31.4 %copy-start.14 = (s32[32,32]{1,0:T(8,128)S(1)}, s32[32,32]{1,0:T(8,128)}, u32[]{:S(2)}) copy-start(s32[32,32]{1,0:T(8,128)} %rows_ref.1) | copy-start | bytes 12292
  93.2 22.1 %all-to-all-start.2 = ((bf16[32,32,512]{2,1,0:T(8,128)(2,1)}), bf16[32,32,512]{2,1,0:T(8,128)(2,1)S(1)}, u32[]{:S(2)}, u32[]{:S(2)}) async-start(bf16[32,32,512]{2,1,0:T(8,128)(2,1)} %bitcast.19), calls=%async_computation.2 | async-start | bytes 2097152 | tf_op jit(solution)/shard_map/all_to_all | solution.py:581
  99.8 7.1 %collective-permute-start.1 = (bf16[464,128]{1,0:T(8,128)(2,1)S(1)}, bf16[464,128]{1,0:T(8,128)(2,1)S(1)}, u32[]{:S(2)}, u32[]{:S(2)}) collective-permute-start(bf16[464,128]{1,0:T(8,128)(2,1)S(1)} %get-tuple-element.39), channel_id=1, source_target_pairs={{0,1},{1,2},{2,3},{3,0},{4,5},{5,6},{6,7},{7,4},{8,9},{9,10},{10,1... | collective-permute-start | bytes 356360 | tf_op jit(solution)/shard_map/ppermute | solution.py:591
  101.5 8.9 %collective-permute-start.2 = (bf16[464,128]{1,0:T(8,128)(2,1)S(1)}, bf16[464,128]{1,0:T(8,128)(2,1)S(1)}, u32[]{:S(2)}, u32[]{:S(2)}) collective-permute-start(bf16[464,128]{1,0:T(8,128)(2,1)S(1)} %get-tuple-element.39), channel_id=1, source_target_pairs={{0,2},{1,3},{2,0},{3,1},{4,6},{5,7},{6,4},{7,5},{8,10},{9,11},{10,... | collective-permute-start | bytes 356360 | tf_op jit(solution)/shard_map/ppermute | solution.py:591
  104.8 5.6 %collective-permute-start.3 = (bf16[464,128]{1,0:T(8,128)(2,1)S(1)}, bf16[464,128]{1,0:T(8,128)(2,1)S(1)}, u32[]{:S(2)}, u32[]{:S(2)}) collective-permute-start(bf16[464,128]{1,0:T(8,128)(2,1)S(1)} %get-tuple-element.39), channel_id=1, source_target_pairs={{0,3},{1,0},{2,1},{3,2},{4,7},{5,4},{6,5},{7,6},{8,11},{9,8},{10,9... | collective-permute-start | bytes 356360 | tf_op jit(solution)/shard_map/ppermute | solution.py:591

commit v2 on v1

--- a/solution.py
+++ b/solution.py
@@ -10,10 +10,9 @@
 bf16 = jnp.bfloat16
 NT = (((1,), (1,)), ((), ()))
 TN = (((0,), (0,)), ((), ()))
-MAIN_LIMIT = 50
+MAIN_LIMIT = 48
 BEFORE_LIMIT = 60
 CHUNK = 1024
-PART = bf16
 KEPT = bf16
 
 
@@ -103,6 +102,10 @@
         copy.wait()
 
 
+def marks_of(remote, n, width):
+    return (remote, remote + n, remote + n + width, remote + n + 2 * width)
+
+
 def before_kernel(
     snd_ref,
     rcv_ref,
@@ -110,14 +113,17 @@
     nodes_ref,
     ein_ref,
     ebias_ref,
-    part_ref,
-    local_ref,
-    far_ref,
-    rcv_n_ref,
+    eout_ref,
+    nin_ref,
+    nout_ref,
+    out_ref,
     table_scr,
 ):
     n, width = nodes_ref.shape
-    remote = far_ref.shape[1]
+    chunk = out_ref.shape[0]
+    remote = out_ref.shape[1] - n - 2 * width - 3 * (width // 2)
+    half = width // 2
+    marks = marks_of(remote, n, width)
     c = pl.program_id(0)
 
     @pl.when(c == 0)
@@ -126,12 +132,27 @@
 
     snd = columns(snd_ref[pl.ds(c, 1), :])
     near = one_hot(columns(rcv_ref[pl.ds(c, 1), :]), 0, n)
-    rcv_n_ref[...] = near
-    local_ref[...] = mm(one_hot(snd, 0, n), nodes_ref[...]).astype(bf16)
-    far_ref[...] = one_hot(snd, n, remote)
-    part_ref[...] = (
+    out_ref[:, :remote] = one_hot(snd, n, remote)
+    out_ref[:, marks[0] : marks[1]] = near
+    out_ref[:, marks[1] : marks[2]] = mm(one_hot(snd, 0, n), nodes_ref[...]).astype(bf16)
+    out_ref[:, marks[2] : marks[3]] = (
         mm(edges_ref[...], ein_ref[:width, :]) + mm(near, table_scr[...]) + ebias_ref[...]
-    ).astype(part_ref.dtype)
+    ).astype(bf16)
+    weights = out_ref.at[:, pl.ds(marks[3], 3 * half)]
+
+    @pl.when(c == 0)
+    def _():
+        weights[:, :half] = nin_ref[:, :half]
+        for k, ref in ((1, eout_ref), (2, ein_ref.at[pl.ds(width, width)])):
+            weights[:width, k * half : (k + 1) * half] = ref[:, :half]
+            weights[width:, k * half : (k + 1) * half] = ref[:, half:]
+
+    @pl.when(c == 1)
+    def _():
+        weights[:, :half] = nin_ref[:, half:]
+        for k, ref in ((1, nout_ref), (2, ein_ref.at[pl.ds(2 * width, width)])):
+            weights[:width, k * half : (k + 1) * half] = ref[:, :half]
+            weights[width:, k * half : (k + 1) * half] = ref[:, half:]
 
 
 def deal(core, mats_ref, vecs, mine_ref, send_ref):
@@ -157,18 +178,11 @@
     nbias_ref,
     ngain_ref,
     arrived_ref,
-    part_hbm,
-    local_hbm,
-    far_hbm,
-    rcv_n_hbm,
+    ready_hbm,
     cot_hbm,
     edges_hbm,
     nodes_hbm,
     ncot_hbm,
-    ein_hbm,
-    eout_hbm,
-    nin_hbm,
-    nout_hbm,
     hg_ref,
     base_ref,
     mine_ref,
@@ -197,11 +211,14 @@
     n = ncot_ref.shape[0]
     chunk = min(CHUNK, count)
     n_chunks = count // chunk
+    remote = far_ref.shape[1]
+    half = width // 2
+    marks = marks_of(remote, n, width)
     streams = [
-        (far_hbm, far_ref),
-        (local_hbm, x_ref.at[:, pl.ds(width, width)]),
-        (part_hbm, part_ref),
-        (rcv_n_hbm, x_ref.at[:, pl.ds(2 * width, n)]),
+        (ready_hbm.at[:, pl.ds(0, remote)], far_ref),
+        (ready_hbm.at[:, pl.ds(marks[1], width)], x_ref.at[:, pl.ds(width, width)]),
+        (ready_hbm.at[:, pl.ds(marks[2], width)], part_ref),
+        (ready_hbm.at[:, pl.ds(marks[0], n)], x_ref.at[:, pl.ds(2 * width, n)]),
         (cot_hbm, cot_ref),
         (edges_hbm, x_ref.at[:, pl.ds(0, width)]),
     ]
@@ -211,32 +228,45 @@
         at = pl.ds(c * chunk, chunk)
         return pltpu.make_async_copy(src.at[at], dst.at[at], chunk_sems.at[k, c])
 
-    singles = [
-        (ein_hbm.at[pl.ds(width, width)], ws_ref),
-        (eout_hbm, eout_ref),
-        (nodes_hbm, node_in_ref.at[:, pl.ds(0, width)]),
-        (nin_hbm, nin_ref),
-        (nout_hbm, nout_ref),
-        (ncot_hbm, ncot_ref),
-        (ein_hbm.at[pl.ds(2 * width, width)], wr_ref),
-    ]
+    def halves(k, first, ref):
+        size = ref.shape[0]
+        return [
+            (
+                ready_hbm.at[pl.ds(first + h * size, size), pl.ds(marks[3] + k * half, half)],
+                ref.at[:, pl.ds(h * half, half)],
+            )
+            for h in range(2)
+        ]
+
+    singles = (
+        halves(2, 0, ws_ref)
+        + halves(1, 0, eout_ref)
+        + [(nodes_hbm, node_in_ref.at[:, pl.ds(0, width)])]
+        + halves(0, 0, nin_ref)
+        + halves(1, 2 * width, nout_ref)
+        + [(ncot_hbm, ncot_ref)]
+        + halves(2, 2 * width, wr_ref)
+    )
     single = [pltpu.make_async_copy(src, dst, sems.at[k]) for k, (src, dst) in enumerate(singles)]
     stream(0, 0).start()
     stream(1, 0).start()
     single[0].start()
+    single[1].start()
     stream(2, 0).start()
-    single[1].start()
+    single[2].start()
+    single[3].start()
     for c in range(1, n_chunks):
         for k in range(3):
             stream(k, c).start()
     for c in range(n_chunks):
         stream(3, c).start()
-    for k in range(2, 6):
+    for k in range(4, 10):
         single[k].start()
     for c in range(n_chunks):
         for k in range(4, 6):
             stream(k, c).start()
-    single[6].start()
+    single[10].start()
+    single[11].start()
 
     egain = egain_ref[...]
 
@@ -282,17 +312,19 @@
         stream(2, c).wait()
         if c == 0:
             single[0].wait()
+            single[1].wait()
 
     def wait_message(c):
         if c == 0:
-            single[1].wait()
+            single[2].wait()
+            single[3].wait()
 
     skewed([pick, activate, send_message], [wait_pick, wait_activate, wait_message])
     for c in range(n_chunks):
         stream(3, c).wait()
     agg = mm_tn(x_ref[:, 2 * width :], pg_ref[...])
 
-    for k in range(2, 6):
+    for k in range(4, 10):
         single[k].wait()
     node_in_ref[:, width:] = agg.astype(bf16)
     node_in = node_in_ref[...]
@@ -338,7 +370,8 @@
         stream(5, c).wait()
     by_inputs = mm_tn(x_ref[...], hg_ref[...])
 
-    single[6].wait()
+    single[10].wait()
+    single[11].wait()
     received = by_inputs[2 * width :].astype(bf16)
     base_ref[...] = (
         upstream + node_in_grad[:, :width] + mm_nt(received, wr_ref[...])
@@ -445,7 +478,7 @@
         out_shape=shape((remote, width), bf16),
         scratch_shapes=[
             pltpu.VMEM((remote, width), bf16),
-            pltpu.SemaphoreType.DMA((4,)),
+            pltpu.SemaphoreType.DMA((2,)),
         ],
         compiler_params=params(58),
         cost_estimate=cost(2 * remote * n * width, 4 * remote * width),
@@ -454,7 +487,9 @@
         outgoing.reshape(regions, cap, width), "dom", split_axis=0, concat_axis=0, tiled=True
     ).reshape(remote, width)
 
-    hidden_part, local, far, rcv_n = pl.pallas_call(
+    assert n_chunks == 2 and chunk == 2 * width
+    columns_in_all = marks_of(remote, n, width)[3] + 3 * (width // 2)
+    ready = pl.pallas_call(
         before_kernel,
         grid=(n_chunks,),
         in_specs=[
@@ -464,19 +499,12 @@
             whole((n, width)),
             whole(edge_in_w.shape),
             whole((1, width)),
+            whole(edge_out_w.shape),
+            whole(node_in_w.shape),
+            whole(node_out_w.shape),
         ],
-        out_specs=[
-            rows_of(width),
-            rows_of(width),
-            rows_of(remote),
-            rows_of(n),
-        ],
-        out_shape=[
-            shape((count, width), PART),
-            shape((count, width), bf16),
-            shape((count, remote), bf16),
-            shape((count, n), bf16),
-        ],
+        out_specs=rows_of(columns_in_all),
+        out_shape=shape((count, columns_in_all), bf16),
         scratch_shapes=[pltpu.VMEM((n, width), bf16)],
         compiler_params=params(BEFORE_LIMIT),
         cost_estimate=cost(6_000_000_000, 16_000_000),
@@ -487,13 +515,16 @@
         nodes,
         edge_in_w,
         edge_bias.reshape(1, width),
+        edge_out_w,
+        node_in_w,
+        node_out_w,
     )
 
     slab = (share * width + 4 * width) // 128
     dealt = (chips, slab, 128)
     hidden_grad, base, mine, to_other = pl.pallas_call(
         main_kernel,
-        in_specs=[smem] * 2 + [vmem] * 4 + [hbm] * 12,
+        in_specs=[smem] * 2 + [vmem] * 4 + [hbm] * 5,
         out_specs=[vmem] * 4,
         out_shape=[
             shape((count, width), bf16),
@@ -502,7 +533,7 @@
             shape(dealt, bf16),
         ],
         scratch_shapes=[
-            pltpu.VMEM((count, width), PART),
+            pltpu.VMEM((count, width), bf16),
             pltpu.VMEM((count, remote), bf16),
             pltpu.VMEM((count, 2 * width + n), bf16),
             pltpu.VMEM((count, width), bf16),
@@ -520,7 +551,7 @@
             pltpu.VMEM((rows, width), bf16),
             pltpu.VMEM((count, width), bf16),
             pltpu.SemaphoreType.DMA((6, n_chunks)),
-            pltpu.SemaphoreType.DMA((7,)),
+            pltpu.SemaphoreType.DMA((12,)),
         ],
         compiler_params=params(MAIN_LIMIT),
         cost_estimate=cost(16_000_000_000, 30_000_000),
@@ -531,18 +562,11 @@
         node_bias.reshape(1, width),
         node_gain.reshape(1, width),
         arrived,
-        hidden_part,
-        local,
-        far,
-        rcv_n,
+        ready,
         cots,
         edges,
         nodes,
         node_cot[0],
-        edge_in_w,
-        edge_out_w,
-        node_in_w,
-        node_out_w,
     )
 
     w_s = edge_in_w[width : 2 * width]

time: 117 us -> 115 us (0.983)
  waiting for transfers between devices: 39.5 us -> 37.5 us
  Pallas kernels: 41.8 us -> 43.4 us
  other arithmetic: 3.31 us -> 1.88 us
    pallas_call x1, Pallas kernels: 7.39 us -> 9.19 us  [shards(): pl.pallas_call(before_kernel, grid=(n_chunks,), in_specs=[whole((n_chunks...]
    all_to_all x1, waiting for transfers between devices: 7.81 us -> 6.03 us  [shards(): lax.all_to_all(outgoing.reshape(regions, cap, width), 'dom', split_axis=0...]
    convert_element_type x1, other arithmetic: 3.31 us -> 1.88 us  [shards(): chip_sum = (mine.astype(f32) + from_other.astype(f32)).astype(bf16)]
    unnamed x32 -> x28, local copies, waits for them, and re-layouts: 4.03 us -> 4.01 us
  transfers between devices with their start and end apart: 7 -> 7, of which waited for: 6 -> 6; matrix products, arithmetic and copies ran while one was open for 2% -> 2% of each run, Pallas kernels for 14% -> 16%
where the time goes in v2:
time: 115 us
  Pallas kernels  43.4 us (38%)
  waiting for transfers between devices  37.5 us (33%)
  starting transfers between devices  24.3 us (21%)
  local copies, waits for them, and re-layouts  6.39 us (6%)
  other arithmetic  1.88 us (2%)
  between operations  1.47 us (1%)
    pallas_call x1, Pallas kernels, shards(): pl.pallas_call(main_kernel, in_specs=[smem] * 2 + [vmem] * 4 + [hbm] * 5,...  21.7 us
    all_to_all x1, waiting for transfers between devices, shards(): lax.all_to_all(chip_sum, 'dom', split_axis=0, concat_axis=0, axis_index_g...  19.1 us
    pallas_call x1, Pallas kernels, shards(): pl.pallas_call(before_kernel, grid=(n_chunks,), in_specs=[whole((n_chunks...  9.19 us
    all_to_all x1, starting transfers between devices, shards(): lax.all_to_all(outgoing.reshape(regions, cap, width), 'dom', split_axis=0...  8.6 us
    all_to_all x1, waiting for transfers between devices, shards(): lax.all_to_all(outgoing.reshape(regions, cap, width), 'dom', split_axis=0...  6.03 us
    ppermute x3, starting transfers between devices, shards(): lax.ppermute(total_bf16, 'rep', [(i, (i + k) % reps) for i in range(reps)])  5.74 us
    all_to_all x1, starting transfers between devices, shards(): lax.all_to_all(sent.reshape(regions, cap, width), 'dom', split_axis=0, co...  4.91 us
    ppermute x3, waiting for transfers between devices, shards(): lax.ppermute(total_bf16, 'rep', [(i, (i + k) % reps) for i in range(reps)])  4.73 us
  transfers between devices with their start and end apart: 7, of which 6 were waited for; matrix products, arithmetic and copies ran while one was open for 2% of the time, Pallas kernels for 16%

profile of v2, /device:TPU:1, one launch (start us, length us, event | category | flops | bytes accessed | tf_op | source)
XLA Modules:
  0.0 114.9 jit_solution(15988600990660907695)
XLA Ops:
  0.7 2.4 %shard_map.183 = bf16[1024,512]{1,0:T(8,128)(2,1)} custom-call(s32[32,32]{1,0:T(8,128)} %rows_ref.1, bf16[256,512]{1,0:T(8,128)(2,1)} %bitcast.21), custom_call_target="tpu_custom_call" | custom-call | flops 268435456 | bytes 2097152 | tf_op jit(solution)/shard_map/pallas_call | solution.py:475
  3.0 8.6 %all-to-all-start = ((bf16[32,32,512]{2,1,0:T(8,128)(2,1)}), bf16[32,32,512]{2,1,0:T(8,128)(2,1)S(1)}, u32[]{:S(2)}, u32[]{:S(2)}) async-start(bf16[32,32,512]{2,1,0:T(8,128)(2,1)} %bitcast.29), calls=%async_computation | async-start | bytes 2097152 | tf_op jit(solution)/shard_map/all_to_all | solution.py:486
  13.6 9.2 %shard_map.184.ready_hbm = bf16[2048,3072]{1,0:T(8,128)(2,1)} custom-call(s32[2,1024]{1,0:T(2,128)} %reshape.54.snd_ref, s32[2,1024]{1,0:T(2,128)} %reshape.55.rcv_ref, bf16[2048,512]{1,0:T(8,128)(2,1)} %bitcast.32, bf16[256,512]{1,0:T(8,128)(2,1)} %bitcast.22, bf16[1536,512]{1,0:T(8,128)(2,1)} %w_ref.1, f32[1,512]{1,0:T(1,128)} %bitcast.34, ...), custom_call_target="tpu_custom_call" | custom-call | flops 6000000000 | bytes 16000000 | tf_op jit(solution)/shard_map/pallas_call | solution.py:492
  22.8 6.0 %all-to-all-done = bf16[32,32,512]{2,1,0:T(8,128)(2,1)S(1)} async-done(((bf16[32,32,512]{2,1,0:T(8,128)(2,1)}), bf16[32,32,512]{2,1,0:T(8,128)(2,1)S(1)}, u32[]{:S(2)}, u32[]{:S(2)}) %all-to-all-start) | async-done | bytes 1048608 | tf_op jit(solution)/shard_map/all_to_all | solution.py:486
  28.8 21.7 %shard_map.185 = (bf16[2048,512]{1,0:T(8,128)(2,1)}, f32[256,512]{1,0:T(8,128)S(1)}, bf16[16,464,128]{2,1,0:T(8,128)(2,1)S(1)}, bf16[16,464,128]{2,1,0:T(8,128)(2,1)S(1)}) custom-call(s32[1]{0:T(128)} %bitcast.place_ref, s32[1]{0:T(128)S(6)} %copy.20.live_ref, f32[1,512]{1,0:T(1,128)S(1)} %bitcast.26, f32[1,512]{1,0:T(1,128)S(1)} %bitcast.27, ...), custom_call_target="tpu_custom_call" | custom-call | flops 16000000000 | bytes 30000000 | tf_op jit(solution)/shard_map/pallas_call | solution.py:525
  51.0 3.5 %collective-permute-done = bf16[16,464,128]{2,1,0:T(8,128)(2,1)S(1)} collective-permute-done((bf16[16,464,128]{2,1,0:T(8,128)(2,1)S(1)}, bf16[16,464,128]{2,1,0:T(8,128)(2,1)S(1)}, u32[]{:S(2)}, u32[]{:S(2)}) %collective-permute-start) | collective-permute-done | bytes 1900576 | tf_op jit(solution)/shard_map/ppermute | solution.py:573
  54.5 1.9 %add_convert_fusion = bf16[16,464,128]{2,1,0:T(8,128)(2,1)} fusion(bf16[16,464,128]{2,1,0:T(8,128)(2,1)S(1)} %collective-permute-done, bf16[16,464,128]{2,1,0:T(8,128)(2,1)S(1)} %get-tuple-element.19), kind=kLoop, calls=%fused_computation | loop fusion | flops 3801088 | bytes 5701632 | tf_op jit(solution)/shard_map/convert_element_type | solution.py:574
  56.4 4.6 %all-to-all-start.1 = ((bf16[16,464,128]{2,1,0:T(8,128)(2,1)}), bf16[16,464,128]{2,1,0:T(8,128)(2,1)}, u32[]{:S(2)}, u32[]{:S(2)}) async-start(bf16[16,464,128]{2,1,0:T(8,128)(2,1)} %add_convert_fusion), calls=%async_computation.1 | async-start | bytes 3801088 | tf_op jit(solution)/shard_map/all_to_all | solution.py:576
  61.0 1.1 slice.3.ws_ref
  62.1 1.4 %copy-done.1 = bf16[1536,512]{1,0:T(8,128)(2,1)S(1)} copy-done((bf16[1536,512]{1,0:T(8,128)(2,1)S(1)}, bf16[1536,512]{1,0:T(8,128)(2,1)}, u32[]{:S(2)}) %copy-start.1) | copy-done | bytes 1572888
  63.5 1.6 %copy-done.2 = bf16[1,2048,512]{2,1,0:T(8,128)(2,1)S(1)} copy-done((bf16[1,2048,512]{2,1,0:T(8,128)(2,1)S(1)}, bf16[1,2048,512]{2,1,0:T(8,128)(2,1)}, u32[]{:S(2)}) %copy-start.2) | copy-done | bytes 2097176
  65.1 2.5 %shard_map.187 = bf16[2048,512]{1,0:T(8,128)(2,1)} custom-call(bf16[2048,512]{1,0:T(8,128)(2,1)S(1)} %copy-done, bf16[2048,512]{1,0:T(8,128)(2,1)S(1)} %bitcast.18, bf16[1536,512]{1,0:T(8,128)(2,1)S(1)} %copy-done.1), custom_call_target="tpu_custom_call" | custom-call | flops 1000 | bytes 1000 | tf_op jit(solution)/shard_map/pallas_call | solution.py:590
  67.6 3.7 %shard_map.186 = (bf16[1024,512]{1,0:T(8,128)(2,1)S(1)}, f32[256,512]{1,0:T(8,128)S(1)}) custom-call(s32[1,2048]{1,0:T(1,128)S(1)} %bitcast.24, bf16[2048,512]{1,0:T(8,128)(2,1)S(1)} %copy-done, bf16[512,512]{1,0:T(8,128)(2,1)S(1)} %slice.3.ws_ref, f32[256,512]{1,0:T(8,128)S(1)} %copy-done.5), custom_call_target="tpu_custom_call" | custom-call | flops 1000 | bytes 1000 | tf_op jit(solution)/shard_map/pallas_call | solution.py:584
  71.3 1.0 copy-done.3
  72.3 19.1 %all-to-all-done.1.parts_ref = bf16[16,464,128]{2,1,0:T(8,128)(2,1)} async-done(((bf16[16,464,128]{2,1,0:T(8,128)(2,1)}), bf16[16,464,128]{2,1,0:T(8,128)(2,1)}, u32[]{:S(2)}, u32[]{:S(2)}) %all-to-all-start.1) | async-done | bytes 1900576 | tf_op jit(solution)/shard_map/all_to_all | solution.py:576
  91.3 4.9 %all-to-all-start.2 = ((bf16[32,32,512]{2,1,0:T(8,128)(2,1)}), bf16[32,32,512]{2,1,0:T(8,128)(2,1)S(1)}, u32[]{:S(2)}, u32[]{:S(2)}) async-start(bf16[32,32,512]{2,1,0:T(8,128)(2,1)} %bitcast.19), calls=%async_computation.2 | async-start | bytes 2097152 | tf_op jit(solution)/shard_map/all_to_all | solution.py:605
  96.3 1.8 %shard_map.189 = (f32[464,128]{1,0:T(8,128)S(1)}, bf16[464,128]{1,0:T(8,128)(2,1)S(1)}) custom-call(bf16[16,464,128]{2,1,0:T(8,128)(2,1)} %all-to-all-done.1.parts_ref), custom_call_target="tpu_custom_call" | custom-call | flops 1000000 | bytes 2000000 | tf_op jit(solution)/shard_map/pallas_call | solution.py:608
  98.0 1.7 %collective-permute-start.1 = (bf16[464,128]{1,0:T(8,128)(2,1)S(1)}, bf16[464,128]{1,0:T(8,128)(2,1)S(1)}, u32[]{:S(2)}, u32[]{:S(2)}) collective-permute-start(bf16[464,128]{1,0:T(8,128)(2,1)S(1)} %get-tuple-element.31), channel_id=1, source_target_pairs={{0,1},{1,2},{2,3},{3,0},{4,5},{5,6},{6,7},{7,4},{8,9},{9,10},{10,1... | collective-permute-start | bytes 356360 | tf_op jit(solution)/shard_map/ppermute | solution.py:615
  99.7 3.3 %collective-permute-start.2 = (bf16[464,128]{1,0:T(8,128)(2,1)S(1)}, bf16[464,128]{1,0:T(8,128)(2,1)S(1)}, u32[]{:S(2)}, u32[]{:S(2)}) collective-permute-start(bf16[464,128]{1,0:T(8,128)(2,1)S(1)} %get-tuple-element.31), channel_id=1, source_target_pairs={{0,2},{1,3},{2,0},{3,1},{4,6},{5,7},{6,4},{7,5},{8,10},{9,11},{10,... | collective-permute-start | bytes 356360 | tf_op jit(solution)/shard_map/ppermute | solution.py:615
  103.9 1.3 %collective-permute-done.1.refs_1_ = bf16[464,128]{1,0:T(8,128)(2,1)S(1)} collective-permute-done((bf16[464,128]{1,0:T(8,128)(2,1)S(1)}, bf16[464,128]{1,0:T(8,128)(2,1)S(1)}, u32[]{:S(2)}, u32[]{:S(2)}) %collective-permute-start.1) | collective-permute-done | bytes 118816 | tf_op jit(solution)/shard_map/ppermute | solution.py:615
  105.2 3.4 %collective-permute-done.2.refs_2_ = bf16[464,128]{1,0:T(8,128)(2,1)S(1)} collective-permute-done((bf16[464,128]{1,0:T(8,128)(2,1)S(1)}, bf16[464,128]{1,0:T(8,128)(2,1)S(1)}, u32[]{:S(2)}, u32[]{:S(2)}) %collective-permute-start.2) | collective-permute-done | bytes 118816 | tf_op jit(solution)/shard_map/ppermute | solution.py:615
  108.6 0.8 shard_map.190
  109.3 4.2 %all-to-all-done.2 = bf16[32,32,512]{2,1,0:T(8,128)(2,1)S(1)} async-done(((bf16[32,32,512]{2,1,0:T(8,128)(2,1)}), bf16[32,32,512]{2,1,0:T(8,128)(2,1)S(1)}, u32[]{:S(2)}, u32[]{:S(2)}) %all-to-all-start.2) | async-done | bytes 1048608 | tf_op jit(solution)/shard_map/all_to_all | solution.py:605
  113.5 1.4 %shard_map.188 = bf16[256,512]{1,0:T(8,128)(2,1)} custom-call(s32[1,1024]{1,0:T(1,128)S(1)} %reshape.47.rows_ref, bf16[1024,512]{1,0:T(8,128)(2,1)S(1)} %bitcast.16, bf16[512,512]{1,0:T(8,128)(2,1)S(1)} %slice.3.ws_ref, f32[256,512]{1,0:T(8,128)S(1)} %get-tuple-element.27.base_ref), custom_call_target="tpu_custom_call" | custom-call | flops 1000 | bytes 1000 | tf_op jit(solution)/shard_map/pallas_call | solution.py:618
  (31 shorter events, 2.6 us)
Async XLA Ops:
  0.6 11.0 %copy-start.7 = (s32[2048]{0:T(1024)S(1)}, s32[2048]{0:T(1024)}, u32[]{:S(2)}) copy-start(s32[2048]{0:T(1024)} %param.28) | copy-start | bytes 24580
  0.6 11.6 %copy-start.13 = (s32[2048]{0:T(1024)S(1)}, s32[2048]{0:T(1024)}, u32[]{:S(2)}) copy-start(s32[2048]{0:T(1024)} %param.29) | copy-start | bytes 24580
  3.0 25.8 %all-to-all-start = ((bf16[32,32,512]{2,1,0:T(8,128)(2,1)}), bf16[32,32,512]{2,1,0:T(8,128)(2,1)S(1)}, u32[]{:S(2)}, u32[]{:S(2)}) async-start(bf16[32,32,512]{2,1,0:T(8,128)(2,1)} %bitcast.29), calls=%async_computation | async-start | bytes 2097152 | tf_op jit(solution)/shard_map/all_to_all | solution.py:486
  13.5 15.3 %copy-start.6 = (bf16[1,256,512]{2,1,0:T(8,128)(2,1)S(1)}, bf16[1,256,512]{2,1,0:T(8,128)(2,1)}, u32[]{:S(2)}) copy-start(bf16[1,256,512]{2,1,0:T(8,128)(2,1)} %param.16) | copy-start | bytes 786436
  13.5 15.3 %copy-start.8 = (bf16[1,256,512]{2,1,0:T(8,128)(2,1)S(1)}, bf16[1,256,512]{2,1,0:T(8,128)(2,1)}, u32[]{:S(2)}) copy-start(bf16[1,256,512]{2,1,0:T(8,128)(2,1)} %param.18) | copy-start | bytes 786436
  13.5 15.3 %copy-start.9 = (f32[512]{0:T(512)S(1)}, f32[512]{0:T(512)}, u32[]{:S(2)}) copy-start(f32[512]{0:T(512)} %param.23) | copy-start | bytes 6148
  13.6 15.3 %copy-start.10 = (f32[512]{0:T(512)S(1)}, f32[512]{0:T(512)}, u32[]{:S(2)}) copy-start(f32[512]{0:T(512)} %param.25) | copy-start | bytes 6148
  13.6 15.3 %copy-start.11 = (f32[512]{0:T(512)S(1)}, f32[512]{0:T(512)}, u32[]{:S(2)}) copy-start(f32[512]{0:T(512)} %param.27) | copy-start | bytes 6148
  50.6 5.9 %copy-start.4 = (f32[256,512]{1,0:T(8,128)}, f32[256,512]{1,0:T(8,128)S(1)}, u32[]{:S(2)}) copy-start(f32[256,512]{1,0:T(8,128)S(1)} %get-tuple-element.24.base_ref) | copy-start | bytes 1572868
  50.6 4.0 %collective-permute-start = (bf16[16,464,128]{2,1,0:T(8,128)(2,1)S(1)}, bf16[16,464,128]{2,1,0:T(8,128)(2,1)S(1)}, u32[]{:S(2)}, u32[]{:S(2)}) collective-permute-start(bf16[16,464,128]{2,1,0:T(8,128)(2,1)S(1)} %get-tuple-element.20), channel_id=1, source_target_pairs={{0,4},{4,0},{8,12},{12,8},{16,20},{20,16},{24,28},{28,24},{32,36},... | collective-permute-start | bytes 5701640 | tf_op jit(solution)/shard_map/ppermute | solution.py:573
  56.4 5.7 %copy-start = (bf16[2048,512]{1,0:T(8,128)(2,1)S(1)}, bf16[2048,512]{1,0:T(8,128)(2,1)}, u32[]{:S(2)}) copy-start(bf16[2048,512]{1,0:T(8,128)(2,1)} %get-tuple-element.23.hg_ref) | copy-start | bytes 6291460
  56.4 34.9 %all-to-all-start.1 = ((bf16[16,464,128]{2,1,0:T(8,128)(2,1)}), bf16[16,464,128]{2,1,0:T(8,128)(2,1)}, u32[]{:S(2)}, u32[]{:S(2)}) async-start(bf16[16,464,128]{2,1,0:T(8,128)(2,1)} %add_convert_fusion), calls=%async_computation.1 | async-start | bytes 3801088 | tf_op jit(solution)/shard_map/all_to_all | solution.py:576
  62.1 1.4 %copy-start.1 = (bf16[1536,512]{1,0:T(8,128)(2,1)S(1)}, bf16[1536,512]{1,0:T(8,128)(2,1)}, u32[]{:S(2)}) copy-start(bf16[1536,512]{1,0:T(8,128)(2,1)} %w_ref.1) | copy-start | bytes 4718596
  63.5 1.6 %copy-start.2 = (bf16[1,2048,512]{2,1,0:T(8,128)(2,1)S(1)}, bf16[1,2048,512]{2,1,0:T(8,128)(2,1)}, u32[]{:S(2)}) copy-start(bf16[1,2048,512]{2,1,0:T(8,128)(2,1)} %param.19) | copy-start | bytes 6291460
  65.1 2.5 %copy-start.5 = (f32[256,512]{1,0:T(8,128)S(1)}, f32[256,512]{1,0:T(8,128)}, u32[]{:S(2)}) copy-start(f32[256,512]{1,0:T(8,128)} %copy-done.4) | copy-start | bytes 1572868
  71.3 1.0 copy-start.3
  91.3 12.4 %copy-start.12 = (s32[32,32]{1,0:T(8,128)S(1)}, s32[32,32]{1,0:T(8,128)}, u32[]{:S(2)}) copy-start(s32[32,32]{1,0:T(8,128)} %rows_ref.1) | copy-start | bytes 12292
  91.3 22.2 %all-to-all-start.2 = ((bf16[32,32,512]{2,1,0:T(8,128)(2,1)}), bf16[32,32,512]{2,1,0:T(8,128)(2,1)S(1)}, u32[]{:S(2)}, u32[]{:S(2)}) async-start(bf16[32,32,512]{2,1,0:T(8,128)(2,1)} %bitcast.19), calls=%async_computation.2 | async-start | bytes 2097152 | tf_op jit(solution)/shard_map/all_to_all | solution.py:605
  98.0 7.2 %collective-permute-start.1 = (bf16[464,128]{1,0:T(8,128)(2,1)S(1)}, bf16[464,128]{1,0:T(8,128)(2,1)S(1)}, u32[]{:S(2)}, u32[]{:S(2)}) collective-permute-start(bf16[464,128]{1,0:T(8,128)(2,1)S(1)} %get-tuple-element.31), channel_id=1, source_target_pairs={{0,1},{1,2},{2,3},{3,0},{4,5},{5,6},{6,7},{7,4},{8,9},{9,10},{10,1... | collective-permute-start | bytes 356360 | tf_op jit(solution)/shard_map/ppermute | solution.py:615
  99.7 8.9 %collective-permute-start.2 = (bf16[464,128]{1,0:T(8,128)(2,1)S(1)}, bf16[464,128]{1,0:T(8,128)(2,1)S(1)}, u32[]{:S(2)}, u32[]{:S(2)}) collective-permute-start(bf16[464,128]{1,0:T(8,128)(2,1)S(1)} %get-tuple-element.31), channel_id=1, source_target_pairs={{0,2},{1,3},{2,0},{3,1},{4,6},{5,7},{6,4},{7,5},{8,10},{9,11},{10,... | collective-permute-start | bytes 356360 | tf_op jit(solution)/shard_map/ppermute | solution.py:615
  103.0 5.6 %collective-permute-start.3 = (bf16[464,128]{1,0:T(8,128)(2,1)S(1)}, bf16[464,128]{1,0:T(8,128)(2,1)S(1)}, u32[]{:S(2)}, u32[]{:S(2)}) collective-permute-start(bf16[464,128]{1,0:T(8,128)(2,1)S(1)} %get-tuple-element.31), channel_id=1, source_target_pairs={{0,3},{1,0},{2,1},{3,2},{4,7},{5,4},{6,5},{7,6},{8,11},{9,8},{10,9... | collective-permute-start | bytes 356360 | tf_op jit(solution)/shard_map/ppermute | solution.py:615

commit v3 on v2

--- a/solution.py
+++ b/solution.py
@@ -59,7 +59,7 @@
 
 
 def sigmoid(value):
-    return 0.5 * jnp.tanh(0.5 * value) + 0.5
+    return 1.0 / (1.0 + jnp.exp(-value))
 
 
 def normalise(value, live=None):

time: 115 us -> 116 us (level)
  no operation moved by 1% of the time
where the time goes in v3:
time: 116 us; the launch traced here: 115 us
  Pallas kernels  43.5 us (38%)
  waiting for transfers between devices  37.5 us (32%)
  starting transfers between devices  24.3 us (21%)
  local copies, waits for them, and re-layouts  6.39 us (6%)
  other arithmetic  1.88 us (2%)
  between operations  1.47 us (1%)
    pallas_call x1, Pallas kernels, shards(): pl.pallas_call(main_kernel, in_specs=[smem] * 2 + [vmem] * 4 + [hbm] * 5,...  21.8 us
    all_to_all x1, waiting for transfers between devices, shards(): lax.all_to_all(chip_sum, 'dom', split_axis=0, concat_axis=0, axis_index_g...  19.1 us
    pallas_call x1, Pallas kernels, shards(): pl.pallas_call(before_kernel, grid=(n_chunks,), in_specs=[whole((n_chunks...  9.19 us
    all_to_all x1, starting transfers between devices, shards(): lax.all_to_all(outgoing.reshape(regions, cap, width), 'dom', split_axis=0...  8.6 us
    all_to_all x1, waiting for transfers between devices, shards(): lax.all_to_all(outgoing.reshape(regions, cap, width), 'dom', split_axis=0...  6.03 us
    ppermute x3, starting transfers between devices, shards(): lax.ppermute(total_bf16, 'rep', [(i, (i + k) % reps) for i in range(reps)])  5.74 us
    all_to_all x1, starting transfers between devices, shards(): lax.all_to_all(sent.reshape(regions, cap, width), 'dom', split_axis=0, co...  4.91 us
    ppermute x3, waiting for transfers between devices, shards(): lax.ppermute(total_bf16, 'rep', [(i, (i + k) % reps) for i in range(reps)])  4.73 us
  transfers between devices with their start and end apart: 7, of which 6 were waited for; matrix products, arithmetic and copies ran while one was open for 2% of the time, Pallas kernels for 16%

profile of v3, /device:TPU:1, one launch (start us, length us, event | category | flops | bytes accessed | tf_op | source)
XLA Modules:
  0.0 115.0 jit_solution(8672108022317938112)
XLA Ops:
  0.7 2.4 %shard_map.183 = bf16[1024,512]{1,0:T(8,128)(2,1)} custom-call(s32[32,32]{1,0:T(8,128)} %rows_ref.1, bf16[256,512]{1,0:T(8,128)(2,1)} %bitcast.21), custom_call_target="tpu_custom_call" | custom-call | flops 268435456 | bytes 2097152 | tf_op jit(solution)/shard_map/pallas_call | solution.py:475
  3.0 8.6 %all-to-all-start = ((bf16[32,32,512]{2,1,0:T(8,128)(2,1)}), bf16[32,32,512]{2,1,0:T(8,128)(2,1)S(1)}, u32[]{:S(2)}, u32[]{:S(2)}) async-start(bf16[32,32,512]{2,1,0:T(8,128)(2,1)} %bitcast.29), calls=%async_computation | async-start | bytes 2097152 | tf_op jit(solution)/shard_map/all_to_all | solution.py:486
  13.6 9.2 %shard_map.184.ready_hbm = bf16[2048,3072]{1,0:T(8,128)(2,1)} custom-call(s32[2,1024]{1,0:T(2,128)} %reshape.54.snd_ref, s32[2,1024]{1,0:T(2,128)} %reshape.55.rcv_ref, bf16[2048,512]{1,0:T(8,128)(2,1)} %bitcast.32, bf16[256,512]{1,0:T(8,128)(2,1)} %bitcast.22, bf16[1536,512]{1,0:T(8,128)(2,1)} %w_ref.1, f32[1,512]{1,0:T(1,128)} %bitcast.34, ...), custom_call_target="tpu_custom_call" | custom-call | flops 6000000000 | bytes 16000000 | tf_op jit(solution)/shard_map/pallas_call | solution.py:492
  22.8 6.0 %all-to-all-done = bf16[32,32,512]{2,1,0:T(8,128)(2,1)S(1)} async-done(((bf16[32,32,512]{2,1,0:T(8,128)(2,1)}), bf16[32,32,512]{2,1,0:T(8,128)(2,1)S(1)}, u32[]{:S(2)}, u32[]{:S(2)}) %all-to-all-start) | async-done | bytes 1048608 | tf_op jit(solution)/shard_map/all_to_all | solution.py:486
  28.8 21.8 %shard_map.185 = (bf16[2048,512]{1,0:T(8,128)(2,1)}, f32[256,512]{1,0:T(8,128)S(1)}, bf16[16,464,128]{2,1,0:T(8,128)(2,1)S(1)}, bf16[16,464,128]{2,1,0:T(8,128)(2,1)S(1)}) custom-call(s32[1]{0:T(128)} %bitcast.place_ref, s32[1]{0:T(128)S(6)} %copy.20.live_ref, f32[1,512]{1,0:T(1,128)S(1)} %bitcast.26, f32[1,512]{1,0:T(1,128)S(1)} %bitcast.27, ...), custom_call_target="tpu_custom_call" | custom-call | flops 16000000000 | bytes 30000000 | tf_op jit(solution)/shard_map/pallas_call | solution.py:525
  51.1 3.5 %collective-permute-done = bf16[16,464,128]{2,1,0:T(8,128)(2,1)S(1)} collective-permute-done((bf16[16,464,128]{2,1,0:T(8,128)(2,1)S(1)}, bf16[16,464,128]{2,1,0:T(8,128)(2,1)S(1)}, u32[]{:S(2)}, u32[]{:S(2)}) %collective-permute-start) | collective-permute-done | bytes 1900576 | tf_op jit(solution)/shard_map/ppermute | solution.py:573
  54.6 1.9 %add_convert_fusion = bf16[16,464,128]{2,1,0:T(8,128)(2,1)} fusion(bf16[16,464,128]{2,1,0:T(8,128)(2,1)S(1)} %collective-permute-done, bf16[16,464,128]{2,1,0:T(8,128)(2,1)S(1)} %get-tuple-element.19), kind=kLoop, calls=%fused_computation | loop fusion | flops 3801088 | bytes 5701632 | tf_op jit(solution)/shard_map/convert_element_type | solution.py:574
  56.5 4.6 %all-to-all-start.1 = ((bf16[16,464,128]{2,1,0:T(8,128)(2,1)}), bf16[16,464,128]{2,1,0:T(8,128)(2,1)}, u32[]{:S(2)}, u32[]{:S(2)}) async-start(bf16[16,464,128]{2,1,0:T(8,128)(2,1)} %add_convert_fusion), calls=%async_computation.1 | async-start | bytes 3801088 | tf_op jit(solution)/shard_map/all_to_all | solution.py:576
  61.1 1.1 slice.3.ws_ref
  62.2 1.4 %copy-done.1 = bf16[1536,512]{1,0:T(8,128)(2,1)S(1)} copy-done((bf16[1536,512]{1,0:T(8,128)(2,1)S(1)}, bf16[1536,512]{1,0:T(8,128)(2,1)}, u32[]{:S(2)}) %copy-start.1) | copy-done | bytes 1572888
  63.6 1.6 %copy-done.2 = bf16[1,2048,512]{2,1,0:T(8,128)(2,1)S(1)} copy-done((bf16[1,2048,512]{2,1,0:T(8,128)(2,1)S(1)}, bf16[1,2048,512]{2,1,0:T(8,128)(2,1)}, u32[]{:S(2)}) %copy-start.2) | copy-done | bytes 2097176
  65.2 2.5 %shard_map.187 = bf16[2048,512]{1,0:T(8,128)(2,1)} custom-call(bf16[2048,512]{1,0:T(8,128)(2,1)S(1)} %copy-done, bf16[2048,512]{1,0:T(8,128)(2,1)S(1)} %bitcast.18, bf16[1536,512]{1,0:T(8,128)(2,1)S(1)} %copy-done.1), custom_call_target="tpu_custom_call" | custom-call | flops 1000 | bytes 1000 | tf_op jit(solution)/shard_map/pallas_call | solution.py:590
  67.7 3.7 %shard_map.186 = (bf16[1024,512]{1,0:T(8,128)(2,1)S(1)}, f32[256,512]{1,0:T(8,128)S(1)}) custom-call(s32[1,2048]{1,0:T(1,128)S(1)} %bitcast.24, bf16[2048,512]{1,0:T(8,128)(2,1)S(1)} %copy-done, bf16[512,512]{1,0:T(8,128)(2,1)S(1)} %slice.3.ws_ref, f32[256,512]{1,0:T(8,128)S(1)} %copy-done.5), custom_call_target="tpu_custom_call" | custom-call | flops 1000 | bytes 1000 | tf_op jit(solution)/shard_map/pallas_call | solution.py:584
  71.4 1.0 copy-done.3
  72.4 19.1 %all-to-all-done.1.parts_ref = bf16[16,464,128]{2,1,0:T(8,128)(2,1)} async-done(((bf16[16,464,128]{2,1,0:T(8,128)(2,1)}), bf16[16,464,128]{2,1,0:T(8,128)(2,1)}, u32[]{:S(2)}, u32[]{:S(2)}) %all-to-all-start.1) | async-done | bytes 1900576 | tf_op jit(solution)/shard_map/all_to_all | solution.py:576
  91.4 4.9 %all-to-all-start.2 = ((bf16[32,32,512]{2,1,0:T(8,128)(2,1)}), bf16[32,32,512]{2,1,0:T(8,128)(2,1)S(1)}, u32[]{:S(2)}, u32[]{:S(2)}) async-start(bf16[32,32,512]{2,1,0:T(8,128)(2,1)} %bitcast.19), calls=%async_computation.2 | async-start | bytes 2097152 | tf_op jit(solution)/shard_map/all_to_all | solution.py:605
  96.4 1.8 %shard_map.189 = (f32[464,128]{1,0:T(8,128)S(1)}, bf16[464,128]{1,0:T(8,128)(2,1)S(1)}) custom-call(bf16[16,464,128]{2,1,0:T(8,128)(2,1)} %all-to-all-done.1.parts_ref), custom_call_target="tpu_custom_call" | custom-call | flops 1000000 | bytes 2000000 | tf_op jit(solution)/shard_map/pallas_call | solution.py:608
  98.1 1.7 %collective-permute-start.1 = (bf16[464,128]{1,0:T(8,128)(2,1)S(1)}, bf16[464,128]{1,0:T(8,128)(2,1)S(1)}, u32[]{:S(2)}, u32[]{:S(2)}) collective-permute-start(bf16[464,128]{1,0:T(8,128)(2,1)S(1)} %get-tuple-element.31), channel_id=1, source_target_pairs={{0,1},{1,2},{2,3},{3,0},{4,5},{5,6},{6,7},{7,4},{8,9},{9,10},{10,1... | collective-permute-start | bytes 356360 | tf_op jit(solution)/shard_map/ppermute | solution.py:615
  99.8 3.3 %collective-permute-start.2 = (bf16[464,128]{1,0:T(8,128)(2,1)S(1)}, bf16[464,128]{1,0:T(8,128)(2,1)S(1)}, u32[]{:S(2)}, u32[]{:S(2)}) collective-permute-start(bf16[464,128]{1,0:T(8,128)(2,1)S(1)} %get-tuple-element.31), channel_id=1, source_target_pairs={{0,2},{1,3},{2,0},{3,1},{4,6},{5,7},{6,4},{7,5},{8,10},{9,11},{10,... | collective-permute-start | bytes 356360 | tf_op jit(solution)/shard_map/ppermute | solution.py:615
  104.0 1.3 %collective-permute-done.1.refs_1_ = bf16[464,128]{1,0:T(8,128)(2,1)S(1)} collective-permute-done((bf16[464,128]{1,0:T(8,128)(2,1)S(1)}, bf16[464,128]{1,0:T(8,128)(2,1)S(1)}, u32[]{:S(2)}, u32[]{:S(2)}) %collective-permute-start.1) | collective-permute-done | bytes 118816 | tf_op jit(solution)/shard_map/ppermute | solution.py:615
  105.3 3.4 %collective-permute-done.2.refs_2_ = bf16[464,128]{1,0:T(8,128)(2,1)S(1)} collective-permute-done((bf16[464,128]{1,0:T(8,128)(2,1)S(1)}, bf16[464,128]{1,0:T(8,128)(2,1)S(1)}, u32[]{:S(2)}, u32[]{:S(2)}) %collective-permute-start.2) | collective-permute-done | bytes 118816 | tf_op jit(solution)/shard_map/ppermute | solution.py:615
  108.7 0.8 shard_map.190
  109.4 4.2 %all-to-all-done.2 = bf16[32,32,512]{2,1,0:T(8,128)(2,1)S(1)} async-done(((bf16[32,32,512]{2,1,0:T(8,128)(2,1)}), bf16[32,32,512]{2,1,0:T(8,128)(2,1)S(1)}, u32[]{:S(2)}, u32[]{:S(2)}) %all-to-all-start.2) | async-done | bytes 1048608 | tf_op jit(solution)/shard_map/all_to_all | solution.py:605
  113.6 1.4 %shard_map.188 = bf16[256,512]{1,0:T(8,128)(2,1)} custom-call(s32[1,1024]{1,0:T(1,128)S(1)} %reshape.47.rows_ref, bf16[1024,512]{1,0:T(8,128)(2,1)S(1)} %bitcast.16, bf16[512,512]{1,0:T(8,128)(2,1)S(1)} %slice.3.ws_ref, f32[256,512]{1,0:T(8,128)S(1)} %get-tuple-element.27.base_ref), custom_call_target="tpu_custom_call" | custom-call | flops 1000 | bytes 1000 | tf_op jit(solution)/shard_map/pallas_call | solution.py:618
  (31 shorter events, 2.6 us)
Async XLA Ops:
  0.6 11.0 %copy-start.7 = (s32[2048]{0:T(1024)S(1)}, s32[2048]{0:T(1024)}, u32[]{:S(2)}) copy-start(s32[2048]{0:T(1024)} %param.28) | copy-start | bytes 24580
  0.6 11.6 %copy-start.13 = (s32[2048]{0:T(1024)S(1)}, s32[2048]{0:T(1024)}, u32[]{:S(2)}) copy-start(s32[2048]{0:T(1024)} %param.29) | copy-start | bytes 24580
  3.0 25.8 %all-to-all-start = ((bf16[32,32,512]{2,1,0:T(8,128)(2,1)}), bf16[32,32,512]{2,1,0:T(8,128)(2,1)S(1)}, u32[]{:S(2)}, u32[]{:S(2)}) async-start(bf16[32,32,512]{2,1,0:T(8,128)(2,1)} %bitcast.29), calls=%async_computation | async-start | bytes 2097152 | tf_op jit(solution)/shard_map/all_to_all | solution.py:486
  13.5 15.3 %copy-start.6 = (bf16[1,256,512]{2,1,0:T(8,128)(2,1)S(1)}, bf16[1,256,512]{2,1,0:T(8,128)(2,1)}, u32[]{:S(2)}) copy-start(bf16[1,256,512]{2,1,0:T(8,128)(2,1)} %param.16) | copy-start | bytes 786436
  13.5 15.3 %copy-start.8 = (bf16[1,256,512]{2,1,0:T(8,128)(2,1)S(1)}, bf16[1,256,512]{2,1,0:T(8,128)(2,1)}, u32[]{:S(2)}) copy-start(bf16[1,256,512]{2,1,0:T(8,128)(2,1)} %param.18) | copy-start | bytes 786436
  13.5 15.3 %copy-start.9 = (f32[512]{0:T(512)S(1)}, f32[512]{0:T(512)}, u32[]{:S(2)}) copy-start(f32[512]{0:T(512)} %param.23) | copy-start | bytes 6148
  13.6 15.3 %copy-start.10 = (f32[512]{0:T(512)S(1)}, f32[512]{0:T(512)}, u32[]{:S(2)}) copy-start(f32[512]{0:T(512)} %param.25) | copy-start | bytes 6148
  13.6 15.3 %copy-start.11 = (f32[512]{0:T(512)S(1)}, f32[512]{0:T(512)}, u32[]{:S(2)}) copy-start(f32[512]{0:T(512)} %param.27) | copy-start | bytes 6148
  50.7 5.9 %copy-start.4 = (f32[256,512]{1,0:T(8,128)}, f32[256,512]{1,0:T(8,128)S(1)}, u32[]{:S(2)}) copy-start(f32[256,512]{1,0:T(8,128)S(1)} %get-tuple-element.24.base_ref) | copy-start | bytes 1572868
  50.7 4.0 %collective-permute-start = (bf16[16,464,128]{2,1,0:T(8,128)(2,1)S(1)}, bf16[16,464,128]{2,1,0:T(8,128)(2,1)S(1)}, u32[]{:S(2)}, u32[]{:S(2)}) collective-permute-start(bf16[16,464,128]{2,1,0:T(8,128)(2,1)S(1)} %get-tuple-element.20), channel_id=1, source_target_pairs={{0,4},{4,0},{8,12},{12,8},{16,20},{20,16},{24,28},{28,24},{32,36},... | collective-permute-start | bytes 5701640 | tf_op jit(solution)/shard_map/ppermute | solution.py:573
  56.5 5.7 %copy-start = (bf16[2048,512]{1,0:T(8,128)(2,1)S(1)}, bf16[2048,512]{1,0:T(8,128)(2,1)}, u32[]{:S(2)}) copy-start(bf16[2048,512]{1,0:T(8,128)(2,1)} %get-tuple-element.23.hg_ref) | copy-start | bytes 6291460
  56.5 34.9 %all-to-all-start.1 = ((bf16[16,464,128]{2,1,0:T(8,128)(2,1)}), bf16[16,464,128]{2,1,0:T(8,128)(2,1)}, u32[]{:S(2)}, u32[]{:S(2)}) async-start(bf16[16,464,128]{2,1,0:T(8,128)(2,1)} %add_convert_fusion), calls=%async_computation.1 | async-start | bytes 3801088 | tf_op jit(solution)/shard_map/all_to_all | solution.py:576
  62.2 1.4 %copy-start.1 = (bf16[1536,512]{1,0:T(8,128)(2,1)S(1)}, bf16[1536,512]{1,0:T(8,128)(2,1)}, u32[]{:S(2)}) copy-start(bf16[1536,512]{1,0:T(8,128)(2,1)} %w_ref.1) | copy-start | bytes 4718596
  63.6 1.6 %copy-start.2 = (bf16[1,2048,512]{2,1,0:T(8,128)(2,1)S(1)}, bf16[1,2048,512]{2,1,0:T(8,128)(2,1)}, u32[]{:S(2)}) copy-start(bf16[1,2048,512]{2,1,0:T(8,128)(2,1)} %param.19) | copy-start | bytes 6291460
  65.2 2.5 %copy-start.5 = (f32[256,512]{1,0:T(8,128)S(1)}, f32[256,512]{1,0:T(8,128)}, u32[]{:S(2)}) copy-start(f32[256,512]{1,0:T(8,128)} %copy-done.4) | copy-start | bytes 1572868
  71.4 1.0 copy-start.3
  91.4 12.4 %copy-start.12 = (s32[32,32]{1,0:T(8,128)S(1)}, s32[32,32]{1,0:T(8,128)}, u32[]{:S(2)}) copy-start(s32[32,32]{1,0:T(8,128)} %rows_ref.1) | copy-start | bytes 12292
  91.4 22.2 %all-to-all-start.2 = ((bf16[32,32,512]{2,1,0:T(8,128)(2,1)}), bf16[32,32,512]{2,1,0:T(8,128)(2,1)S(1)}, u32[]{:S(2)}, u32[]{:S(2)}) async-start(bf16[32,32,512]{2,1,0:T(8,128)(2,1)} %bitcast.19), calls=%async_computation.2 | async-start | bytes 2097152 | tf_op jit(solution)/shard_map/all_to_all | solution.py:605
  98.1 7.2 %collective-permute-start.1 = (bf16[464,128]{1,0:T(8,128)(2,1)S(1)}, bf16[464,128]{1,0:T(8,128)(2,1)S(1)}, u32[]{:S(2)}, u32[]{:S(2)}) collective-permute-start(bf16[464,128]{1,0:T(8,128)(2,1)S(1)} %get-tuple-element.31), channel_id=1, source_target_pairs={{0,1},{1,2},{2,3},{3,0},{4,5},{5,6},{6,7},{7,4},{8,9},{9,10},{10,1... | collective-permute-start | bytes 356360 | tf_op jit(solution)/shard_map/ppermute | solution.py:615
  99.8 8.9 %collective-permute-start.2 = (bf16[464,128]{1,0:T(8,128)(2,1)S(1)}, bf16[464,128]{1,0:T(8,128)(2,1)S(1)}, u32[]{:S(2)}, u32[]{:S(2)}) collective-permute-start(bf16[464,128]{1,0:T(8,128)(2,1)S(1)} %get-tuple-element.31), channel_id=1, source_target_pairs={{0,2},{1,3},{2,0},{3,1},{4,6},{5,7},{6,4},{7,5},{8,10},{9,11},{10,... | collective-permute-start | bytes 356360 | tf_op jit(solution)/shard_map/ppermute | solution.py:615
  103.1 5.6 %collective-permute-start.3 = (bf16[464,128]{1,0:T(8,128)(2,1)S(1)}, bf16[464,128]{1,0:T(8,128)(2,1)S(1)}, u32[]{:S(2)}, u32[]{:S(2)}) collective-permute-start(bf16[464,128]{1,0:T(8,128)(2,1)S(1)} %get-tuple-element.31), channel_id=1, source_target_pairs={{0,3},{1,0},{2,1},{3,2},{4,7},{5,4},{6,5},{7,6},{8,11},{9,8},{10,9... | collective-permute-start | bytes 356360 | tf_op jit(solution)/shard_map/ppermute | solution.py:615
